TPU v7x, 32 devices: a whole 2x2x4 slice. The times are simulated.
32 devices in a mesh: groups: 2 (over x), tile: 16 (over z, y, core).
Axes of the slice: x: 2, y: 2, z: 4, core: 2. Of those that a mesh axis runs over, the one named last changes fastest.
Arguments:
- latent_rows: bfloat16 [4096, 256], P(('groups', 'tile')), parts along dimension 0, may hold values from -6 to 6
- line_order: int32 [128], P('groups'), parts along dimension 0, may hold values from 0 to 63, each once
- conv_weight: bfloat16 [3, 3, 3, 256, 128], replicated, may hold values from -0.078125 to 0.078125
- conv_bias: float32 [128], replicated, may hold values from -3 to 3
- blend_table: float32 [4, 8], replicated, may hold values from 0.25 to 4
- blend_ids: int32 [32], P('groups'), parts along dimension 0, may hold values from 0 to 3
Outputs:
- frames: bfloat16 [16, 32, 64, 128], P('groups', None, 'tile'), parts along dimension 0
There are 2 independent parts, one for each index of `groups`. A program takes and returns all parts, laid end to end along the dimension named above; an argument that names none is the same for every part. Nothing has to cross between parts.
Inputs may be any that keep to these rules, and one draw needn't show every extreme that they name: line_order is a permutation of the 64 latent lines.
All inputs are finite; a program needn't handle non-finite values.
Results may differ from a plain program's by a relative error of at most 0.001.
Values may be sent and summed in bfloat16 or wider, within the bound.
No kernel may reach another device: no remote copies, remote signals or barrier semaphores. Data moves between devices by JAX's collectives and lax.ppermute only.
A program may use at most 64 MiB of HBM per device.

v0:
```python
import jax
import jax.numpy as jnp
from jax import lax
from jax.sharding import PartitionSpec as P

LT = 4
WD = 2


def from_behind(value, axis, steps):
    count = lax.axis_size(axis)
    initial, last = (max(0, -steps), min(count, count - steps))
    return lax.ppermute(value, axis, [(source, source + steps) for source in range(initial, last)])


def upsample(values):
    values = jnp.repeat(values, 2, axis=0)
    values = jnp.repeat(values, 2, axis=1)
    return jnp.repeat(values, 2, axis=2)


def decode_tile(window, conv_weight, conv_bias):
    upsampled = upsample(window)
    upsampled = jnp.concatenate([upsampled[:1], upsampled[:1], upsampled], axis=0)
    output = lax.conv_general_dilated(
        upsampled[None],
        conv_weight,
        (1, 1, 1),
        [(0, 0), (1, 1), (1, 1)],
        dimension_numbers=("NDHWC", "DHWIO", "NDHWC"),
        preferred_element_type=jnp.float32,
    )[0]
    return jax.nn.silu(output + conv_bias)


def blend_profile(blend_table, blend_ids, tile_at):
    kind_index = lax.dynamic_index_in_dim(blend_ids, tile_at, 0, keepdims=False)
    selector = (jnp.arange(blend_table.shape[0], dtype=jnp.int32) == kind_index).astype(jnp.float32)
    return jnp.sum(selector[:, None] * blend_table, axis=0)


def per_device(latent_rows, line_order, conv_weight, conv_bias, blend_table, blend_ids):
    tile_count = lax.axis_size("tile")
    position = lax.axis_index("tile")
    channels = latent_rows.shape[1]
    lines_dev = latent_rows.shape[0] // (WD * tile_count)
    blocks = latent_rows.reshape(lines_dev, tile_count, WD, channels)
    zero_col = jnp.zeros((lines_dev, 1, 1, channels), latent_rows.dtype)
    lower_cols = jnp.concatenate([zero_col, blocks[:, :-1, -1:]], axis=1)
    upper_cols = jnp.concatenate([blocks[:, 1:, :1], zero_col], axis=1)
    widened = jnp.concatenate([lower_cols, blocks, upper_cols], axis=2)
    received = lax.all_to_all(widened, "tile", split_axis=1, concat_axis=0, tiled=True)
    width_now = WD + 2
    line_count = received.shape[0]
    gathered_rows = received.reshape(line_count, width_now, channels)
    inverse = (
        jnp.zeros((line_count,), jnp.int32)
        .at[line_order]
        .set(jnp.arange(line_count, dtype=jnp.int32))
    )
    latent = gathered_rows[inverse].reshape(LT, line_count // LT, width_now, channels)
    decoded = decode_tile(latent, conv_weight, conv_bias)
    lower_at = jnp.maximum(position - 1, 0)
    upper_at = jnp.minimum(position + 1, tile_count - 1)
    has_lower = (position > 0).astype(jnp.float32)
    has_upper = (position < tile_count - 1).astype(jnp.float32)
    weight_self = blend_profile(blend_table, blend_ids, position)
    weight_lower = blend_profile(blend_table, blend_ids, lower_at)
    weight_upper = blend_profile(blend_table, blend_ids, upper_at)
    weighted = decoded * weight_self[None, None, :, None]
    from_lower = from_behind(weighted[:, :, -2:], "tile", 1)
    from_upper = from_behind(weighted[:, :, :2], "tile", -1)
    blended = weighted[:, :, 2:-2]
    blended = blended.at[:, :, :2].add(from_lower)
    blended = blended.at[:, :, -2:].add(from_upper)
    weight_sum = weight_self[2:-2]
    weight_sum = weight_sum.at[:2].add(has_lower * weight_lower[-2:])
    weight_sum = weight_sum.at[-2:].add(has_upper * weight_upper[:2])
    return (blended / weight_sum[None, None, :, None]).astype(jnp.bfloat16)


def solution(mesh):
    return jax.shard_map(
        per_device,
        mesh=mesh,
        in_specs=(P(("groups", "tile"), None), P("groups"), P(), P(), P(), P("groups")),
        out_specs=P("groups", None, "tile", None),
        check_vma=False,
    )
```

profile of v0, /device:TPU:5, one launch (start us, length us, event | category | flops | bytes accessed | tf_op | source)
XLA Modules:
  0.0 53.6 jit_solution(13139769069828558887)
XLA Ops:
  0.0 0.0 copy-start
  0.0 1.0 %reshape.160 = bf16[4,16,2,256]{3,2,1,0:T(2,128)(2,1)S(1)} reshape(bf16[128,256]{1,0:T(8,128)(2,1)} %param.14) | data formatting | bytes 131072 | tf_op jit(solution)/shard_map/reshape | solution.py:47
  1.0 0.1 fusion.11
  1.1 0.9 %fusion.6 = bf16[4,16,4,256]{3,2,0,1:T(4,128)(2,1)} fusion(bf16[4,15,1,256]{3,2,0,1:T(2,128)(2,1)S(1)} %get-tuple-element.59, bf16[4,15,1,256]{3,2,0,1:T(2,128)(2,1)S(1)} %get-tuple-element.58, bf16[4,16,2,256]{3,2,1,0:T(2,128)(2,1)S(1)} %reshape.160), kind=kLoop, calls=%fused_computation.15 | loop fusion | flops 655360 | bytes 258048 | tf_op jit(solution)/shard_map/concatenate | solution.py:51
  2.0 6.7 %all-to-all-start = ((bf16[4,16,4,256]{3,2,0,1:T(4,128)(2,1)}), bf16[4,16,4,256]{3,2,0,1:T(4,128)(2,1)S(1)}, u32[]{:S(2)}, u32[]{:S(2)}) async-start(bf16[4,16,4,256]{3,2,0,1:T(4,128)(2,1)} %fusion.6), calls=%async_computation | async-start | bytes 262144 | tf_op jit(solution)/shard_map/all_to_all | solution.py:52
  8.7 1.4 %fusion.12 = (s32[1]{0:T(128)}, s32[1]{0:T(128)}, s32[1]{0:T(128)}) fusion(s32[16]{0:T(128)} %param.19, s32[]{:T(128)S(6)} %max.3, s32[]{:T(128)S(6)} %select_n.16, s32[]{:T(128)S(6)} %select_n.17), kind=kLoop, calls=%fused_computation.33 | loop fusion | bytes 36 | tf_op jit(solution)/shard_map/jit(dynamic_index_in_dim)/dynamic_slice | solution.py:37
  10.1 0.6 %compare_convert_fusion.2 = f32[4]{0:T(128)S(1)} fusion(s32[]{:T(128)} %bitcast.10), kind=kLoop, calls=%fused_computation.26 | loop fusion | flops 8 | bytes 20 | tf_op jit(solution)/shard_map/convert_element_type | solution.py:38
  10.7 1.2 %compare_convert_fusion = (f32[4]{0:T(128)S(1)}, f32[4]{0:T(128)S(1)}) fusion(s32[]{:T(128)} %bitcast.12, s32[]{:T(128)} %bitcast.11), kind=kLoop, calls=%fused_computation.24 | loop fusion | flops 16 | bytes 40 | tf_op jit(solution)/shard_map/convert_element_type | solution.py:38
  11.9 0.8 %multiply_reduce_fusion = (f32[8]{0:T(128)S(1)}, f32[8]{0:T(128)S(1)}, f32[8]{0:T(128)S(1)}) fusion(f32[4,8]{1,0:T(4,128)} %param.18, f32[4]{0:T(128)S(1)} %get-tuple-element.63, f32[4]{0:T(128)S(1)} %compare_convert_fusion.2, f32[4]{0:T(128)S(1)} %get-tuple-element.64), kind=kLoop, calls=%fused_computation.21 | loop fusion | flops 168 | bytes 272 | tf_op jit(solution)/shard_map/reduce_sum | solution.py:39
  12.7 0.1 slice.131
  12.8 0.7 %compare_select_fusion.1 = s32[64]{0:T(128)S(1)} fusion(s32[64]{0:T(128)} %param.15), kind=kLoop, calls=%fused_computation.20 | loop fusion | flops 192 | bytes 512 | tf_op jit(solution)/shard_map/select_n | solution.py:59
  13.4 0.8 %scatter_custom_fusion = s32[64]{0:T(128)S(1)} fusion(s32[64]{0:T(128)S(1)} %compare_select_fusion.1, s32[64]{0:T(128)S(1)} %iota.18, s32[]{:T(128)} %constant.121.clone.1), kind=kCustom, calls=%fused_computation.29 | custom fusion | bytes 260 | tf_op jit(solution)/shard_map/scatter | solution.py:59
  14.3 0.3 all-to-all-done
  14.6 0.7 %gather_fusion = bf16[64,4,256]{2,1,0:T(4,128)(2,1)S(1)} fusion(bf16[64,4,256]{2,1,0:T(4,128)(2,1)S(1)} %bitcast.24, s32[1024]{0:T(1024)S(1)} %pad_clamp_fusion), kind=kCustom, calls=%fused_computation | custom fusion | bytes 262400 | tf_op jit(solution)/shard_map/gather | solution.py:61
  15.3 0.1 broadcast_in_dim.35
  15.4 0.1 broadcast_in_dim.38
  15.5 0.1 broadcast_in_dim.39
  15.5 0.1 broadcast_in_dim.40
  15.7 1.7 %broadcast_in_dim.41 = bf16[8,32,4,2,256]{4,3,2,1,0:T(2,128)(2,1)} broadcast(bf16[8,32,4,256]{3,2,1,0:T(4,128)(2,1)S(1)} %bitcast.19), dimensions={0,1,2,4} | broadcast | bytes 1572864 | tf_op jit(solution)/shard_map/broadcast_in_dim | solution.py:19
  17.4 1.5 %reshape.165 = bf16[8,32,8,256]{3,2,1,0:T(8,128)(2,1)S(1)} reshape(bf16[8,32,4,2,256]{4,3,2,1,0:T(2,128)(2,1)} %broadcast_in_dim.41) | data formatting | bytes 2097152 | tf_op jit(solution)/shard_map/reshape | solution.py:19
  18.9 0.1 maximum_bitcast_fusion
  19.0 0.0 copy-done
  19.0 0.0 copy-start.1
  19.0 20.3 %fusion = f32[1,8,32,8,128]{4,0,3,2,1:T(1,128)S(1)} fusion(bf16[3,3,3,256,128]{4,3,2,1,0:T(8,128)(2,1)S(1)} %copy-done, bf16[1,10,32,8,256]{4,3,2,1,0:T(8,128)(2,1)S(1)} %maximum_bitcast_fusion), kind=kOutput, calls=%fused_computation.2 | convolution fusion | flops 3252682752 | bytes 4128768 | tf_op jit(solution)/shard_map/conv_general_dilated | solution.py:25
  39.3 0.0 copy-done.1
  39.3 0.3 multiply_multiply_fusion
  39.6 0.9 %fusion.10 = (f32[8,32,2,128]{3,2,1,0:T(2,128)S(1)}, f32[8,32,2,128]{3,2,1,0:T(2,128)}) fusion(f32[8,32,8,128]{3,2,1,0:T(8,128)S(1)} %multiply_multiply_fusion), kind=kLoop, calls=%fused_computation.31 | loop fusion | bytes 1048576 | tf_op jit(solution)/shard_map/slice | solution.py:72
  40.5 3.0 %collective-permute-start = (f32[8,32,2,128]{3,2,1,0:T(2,128)}, f32[8,32,2,128]{3,2,1,0:T(2,128)S(1)}, u32[]{:S(2)}, u32[]{:S(2)}) collective-permute-start(f32[8,32,2,128]{3,2,1,0:T(2,128)} %get-tuple-element.57), channel_id=1, source_target_pairs={{0,1},{1,2},{2,3},{3,4},{4,5},{5,6},{6,7},{7,8},{8,9},{9,10},{10,1... | collective-permute-start | bytes 786440 | tf_op jit(solution)/shard_map/ppermute | solution.py:13
  43.5 0.1 constant_dynamic-update-slice_fusion.1
  43.6 0.2 constant_dynamic-update-slice_fusion
  43.8 0.1 slice.141
  43.9 1.9 %collective-permute-start.1 = (f32[8,32,2,128]{3,2,1,0:T(2,128)S(1)}, f32[8,32,2,128]{3,2,1,0:T(2,128)S(1)}, u32[]{:S(2)}, u32[]{:S(2)}) collective-permute-start(f32[8,32,2,128]{3,2,1,0:T(2,128)S(1)} %get-tuple-element.56), channel_id=1, source_target_pairs={{1,0},{2,1},{3,2},{4,3},{5,4},{6,5},{7,6},{8,7},{9,8},{10,9},{11,1... | collective-permute-start | bytes 786440 | tf_op jit(solution)/shard_map/ppermute | solution.py:13
  45.8 1.3 %collective-permute-done = f32[8,32,2,128]{3,2,1,0:T(2,128)S(1)} collective-permute-done((f32[8,32,2,128]{3,2,1,0:T(2,128)}, f32[8,32,2,128]{3,2,1,0:T(2,128)S(1)}, u32[]{:S(2)}, u32[]{:S(2)}) %collective-permute-start) | collective-permute-done | bytes 262176 | tf_op jit(solution)/shard_map/ppermute | solution.py:13
  47.1 0.2 fusion.3
  47.4 5.1 %collective-permute-done.1 = f32[8,32,2,128]{3,2,1,0:T(2,128)S(1)} collective-permute-done((f32[8,32,2,128]{3,2,1,0:T(2,128)S(1)}, f32[8,32,2,128]{3,2,1,0:T(2,128)S(1)}, u32[]{:S(2)}, u32[]{:S(2)}) %collective-permute-start.1) | collective-permute-done | bytes 262176 | tf_op jit(solution)/shard_map/ppermute | solution.py:13
  52.5 0.3 fusion.2
  52.8 0.9 %divide_convert_fusion = bf16[8,32,4,128]{3,2,1,0:T(4,128)(2,1)} fusion(f32[8,32,4,128]{3,2,1,0:T(4,128)S(1)} %fusion.2, f32[4]{0:T(128)S(1)} %constant_dynamic-update-slice_fusion), kind=kLoop, calls=%fused_computation.6 | loop fusion | flops 262144 | bytes 786448 | tf_op jit(solution)/shard_map/convert_element_type | solution.py:79
  (5 shorter events, 0.0 us)
Async XLA Ops:
  0.0 19.0 %copy-start = (bf16[3,3,3,256,128]{4,3,2,1,0:T(8,128)(2,1)S(1)}, bf16[3,3,3,256,128]{4,3,2,1,0:T(8,128)(2,1)}, u32[]{:S(2)}) copy-start(bf16[3,3,3,256,128]{4,3,2,1,0:T(8,128)(2,1)} %param.16) | copy-start | bytes 5308420
  2.0 12.6 %all-to-all-start = ((bf16[4,16,4,256]{3,2,0,1:T(4,128)(2,1)}), bf16[4,16,4,256]{3,2,0,1:T(4,128)(2,1)S(1)}, u32[]{:S(2)}, u32[]{:S(2)}) async-start(bf16[4,16,4,256]{3,2,0,1:T(4,128)(2,1)} %fusion.6), calls=%async_computation | async-start | bytes 262144 | tf_op jit(solution)/shard_map/all_to_all | solution.py:52
  19.0 20.3 %copy-start.1 = (f32[128]{0:T(128)S(1)}, f32[128]{0:T(128)}, u32[]{:S(2)}) copy-start(f32[128]{0:T(128)} %param.17) | copy-start | bytes 1540
  40.5 6.6 %collective-permute-start = (f32[8,32,2,128]{3,2,1,0:T(2,128)}, f32[8,32,2,128]{3,2,1,0:T(2,128)S(1)}, u32[]{:S(2)}, u32[]{:S(2)}) collective-permute-start(f32[8,32,2,128]{3,2,1,0:T(2,128)} %get-tuple-element.57), channel_id=1, source_target_pairs={{0,1},{1,2},{2,3},{3,4},{4,5},{5,6},{6,7},{7,8},{8,9},{9,10},{10,1... | collective-permute-start | bytes 786440 | tf_op jit(solution)/shard_map/ppermute | solution.py:13
  43.9 8.6 %collective-permute-start.1 = (f32[8,32,2,128]{3,2,1,0:T(2,128)S(1)}, f32[8,32,2,128]{3,2,1,0:T(2,128)S(1)}, u32[]{:S(2)}, u32[]{:S(2)}) collective-permute-start(f32[8,32,2,128]{3,2,1,0:T(2,128)S(1)} %get-tuple-element.56), channel_id=1, source_target_pairs={{1,0},{2,1},{3,2},{4,3},{5,4},{6,5},{7,6},{8,7},{9,8},{10,9},{11,1... | collective-permute-start | bytes 786440 | tf_op jit(solution)/shard_map/ppermute | solution.py:13
where the time goes:
time: 54 us; the launch traced here: 53.6 us
  matrix products  20.3 us (38%)
  starting transfers between devices  11.6 us (21%)
  local copies, waits for them, and re-layouts  8.63 us (16%)
  waiting for transfers between devices  6.73 us (12%)
  other arithmetic  6.2 us (11%)
    conv_general_dilated x1, matrix products, decode_tile(): lax.conv_general_dilated(upsampled[None], conv_weight, (1, 1, 1), [(0, 0)...  20.3 us
    all_to_all x1, starting transfers between devices, per_device(): lax.all_to_all(widened, 'tile', split_axis=1, concat_axis=0, tiled=True)  6.67 us
    ppermute x2, waiting for transfers between devices, from_behind(): lax.ppermute(value, axis, [(source, source + steps) for source in range(i...  6.41 us
    ppermute x2, starting transfers between devices, from_behind(): lax.ppermute(value, axis, [(source, source + steps) for source in range(i...  4.94 us
    broadcast_in_dim x3, local copies, waits for them, and re-layouts, upsample(): return jnp.repeat(values, 2, axis=2)  1.84 us
    convert_element_type x2, other arithmetic, blend_profile(): (jnp.arange(blend_table.shape[0], dtype=jnp.int32) == kind_index).astype(...  1.83 us
    reshape x1, local copies, waits for them, and re-layouts, upsample(): return jnp.repeat(values, 2, axis=2)  1.47 us
    dynamic_slice x1, local copies, waits for them, and re-layouts, blend_profile(): kind_index = lax.dynamic_index_in_dim(blend_ids, tile_at, 0, keepdims=False)  1.42 us
  transfers between devices with their start and end apart: 3, of which 3 were waited for; matrix products, arithmetic and copies ran while one was open for 11% of the time, Pallas kernels for 0%

commit v1 on v0

v1 whole, which is shorter than its diff:
```python
import functools

import jax
import jax.numpy as jnp
from jax import lax
from jax.experimental import pallas as pl
from jax.experimental.pallas import tpu as pltpu
from jax.sharding import PartitionSpec as P

LT = 4
WD = 2
NEIGHBOUR = ((0, 1, None, 2), (1, 1, 2, 2), (1, None, 2, 3))
OWN = ((0, 1, 1, 2), (1, 1, 2, 2), (1, 2, 2, 3))
NONE = 7


def pick(index, values):
    out = jnp.full(index.shape, NONE, jnp.int32)
    for at, value in enumerate(values):
        if value is not None:
            out = jnp.where(index == at, value, out)
    return out


def dot(a, b):
    return jnp.dot(a, b, preferred_element_type=jnp.float32)


def windows_kernel(tiles, x_ref, out_ref):
    rows_in, _ = x_ref.shape
    rows_out = out_ref.shape[0]
    width = tiles * WD
    lines = rows_in // width
    row = lax.broadcasted_iota(jnp.int32, (rows_out, rows_in), 0)
    col = lax.broadcasted_iota(jnp.int32, (rows_out, rows_in), 1)
    span = WD + 2
    tile = row // (lines * span)
    line = (row // span) % lines
    at = tile * WD - 1 + row % span
    hit = (at >= 0) & (at < width) & (line * width + at == col)
    out_ref[...] = dot(hit.astype(jnp.bfloat16), x_ref[...]).astype(jnp.bfloat16)


def select_kernel(tiles, key_ref, ids_ref, table_ref, at_ref, hot_ref, mix_ref):
    rows, cols = hot_ref.shape[1:]
    slot = lax.broadcasted_iota(jnp.int32, (rows, 1), 0)
    key = jnp.broadcast_to(key_ref[...], (rows, cols))
    values = NEIGHBOUR, OWN
    for kw in range(3):
        want = (slot // 8) * 8 + pick(slot % 8, values[0][kw] + values[1][kw])
        hot_ref[kw] = (key == want).astype(jnp.bfloat16)
    at = at_ref[0]
    own = ids_ref[at]
    lower = ids_ref[jnp.maximum(at - 1, 0)]
    upper = ids_ref[jnp.minimum(at + 1, tiles - 1)]
    has_lower = jnp.where(at > 0, 1.0, 0.0)
    has_upper = jnp.where(at < tiles - 1, 1.0, 0.0)
    wide = 2 * WD + 4
    neighbour = [has_lower * table_ref[lower, wide - 2], has_lower * table_ref[lower, wide - 1]]
    neighbour += [has_upper * table_ref[upper, 0], has_upper * table_ref[upper, 1]]
    mine = [table_ref[own, c] for c in range(2, wide - 2)]
    sub = lax.broadcasted_iota(jnp.int32, mix_ref.shape, 0)
    weight = jnp.zeros(mix_ref.shape, jnp.float32)
    total = jnp.ones(mix_ref.shape, jnp.float32)
    for q in range(4):
        weight = jnp.where(sub == q, neighbour[q], weight)
        weight = jnp.where(sub == q + 4, mine[q], weight)
        total = jnp.where(sub % 4 == q, neighbour[q] + mine[q], total)
    mix_ref[...] = weight / total


def decode_kernel(rows_ref, hot_ref, w_ref, bias_ref, mix_ref, out_ref, lhs_ref, part_ref):
    depth = rows_ref.shape[1]
    count = hot_ref.shape[1]
    frame = count // LT
    co = w_ref.shape[1]
    rows = rows_ref[...]
    for kw in range(3):
        lhs_ref[:, kw * depth:(kw + 1) * depth] = dot(hot_ref[kw], rows).astype(jnp.bfloat16)
    taps = [w_ref[k * 3 * depth:(k + 1) * 3 * depth, :] for k in range(9)]
    lhs = lhs_ref[...]
    for k in range(0, 9, 2):
        if k + 1 < 9:
            both = dot(lhs, jnp.concatenate([taps[k], taps[k + 1]], axis=1))
            part_ref[k] = both[:, :co]
            part_ref[k + 1] = both[:, co:]
        else:
            part_ref[k] = dot(lhs, taps[k])
    bias = bias_ref[...]
    mix = jnp.concatenate([mix_ref[...]] * (frame // 8), axis=0)
    low = lax.broadcasted_iota(jnp.int32, (frame, co), 0) % 8 < 4
    zero = jnp.zeros((8, co), jnp.float32)
    before = None
    for t in range(LT):
        now = []
        for kt in range(3):
            p0, p1, p2 = (part_ref[kt * 3 + kh, t * frame:(t + 1) * frame, :] for kh in range(3))
            even = jnp.concatenate([zero, p0[:-8]], axis=0) + (p1 + p2)
            odd = (p0 + p1) + jnp.concatenate([p2[8:], zero], axis=0)
            now.append((even, odd))
        if before is None:
            before = now
        for tp in range(2):
            blended = []
            for hp in range(2):
                middle = before[1][hp] if tp == 0 else now[1][hp]
                value = before[0][hp] + middle + now[2][hp] + bias
                value = value / (1.0 + jnp.exp(-value))
                blended.append(value * mix)
            straight = jnp.where(low, blended[0], blended[1])
            crossed = jnp.where(low, blended[1], blended[0])
            crossed = pltpu.roll(crossed.reshape(frame // 8, 8, co), 4, 1).reshape(frame, co)
            at = (2 * t + tp) * frame
            out_ref[at:at + frame, :] = (straight + crossed).astype(jnp.bfloat16)
        before = now


def vmem():
    return pl.BlockSpec(memory_space=pltpu.VMEM)


def smem():
    return pl.BlockSpec(memory_space=pltpu.SMEM)


def per_device(latent_rows, line_order, conv_weight, conv_bias, blend_table, blend_ids):
    tiles = lax.axis_size("tile")
    rows, depth = latent_rows.shape
    co = conv_weight.shape[-1]
    lines = line_order.shape[0]
    span = WD + 2
    windows = pl.pallas_call(
        functools.partial(windows_kernel, tiles),
        out_shape=jax.ShapeDtypeStruct((lines * span, depth), jnp.bfloat16),
        in_specs=[vmem()],
        out_specs=vmem(),
    )(latent_rows)
    received = lax.all_to_all(windows, "tile", 0, 0, tiled=True)
    key = (line_order[:, None] * 8 + jnp.arange(span, dtype=jnp.int32)[None, :]).reshape(1, lines * span)
    position = lax.axis_index("tile").astype(jnp.int32).reshape(1)
    hot, mix = pl.pallas_call(
        functools.partial(select_kernel, tiles),
        out_shape=(
            jax.ShapeDtypeStruct((3, lines * 8, lines * span), jnp.bfloat16),
            jax.ShapeDtypeStruct((8, co), jnp.float32),
        ),
        in_specs=[vmem(), smem(), smem(), smem()],
        out_specs=(vmem(), vmem()),
    )(key, blend_ids, blend_table, position)
    frame = lines // LT * 8
    out = pl.pallas_call(
        decode_kernel,
        out_shape=jax.ShapeDtypeStruct((2 * LT * frame, co), jnp.bfloat16),
        in_specs=[vmem()] * 5,
        out_specs=vmem(),
        scratch_shapes=[
            pltpu.VMEM((lines * 8, 3 * depth), jnp.bfloat16),
            pltpu.VMEM((9, lines * 8, co), jnp.float32),
        ],
        compiler_params=pltpu.CompilerParams(vmem_limit_bytes=48 * 1024 * 1024),
    )(received, hot, conv_weight.reshape(-1, co), conv_bias.reshape(1, co), mix)
    return out.reshape(2 * LT, lines // LT * 2, 2 * WD, co)


def solution(mesh):
    return jax.shard_map(
        per_device,
        mesh=mesh,
        in_specs=(P(("groups", "tile"), None), P("groups"), P(), P(), P(), P("groups")),
        out_specs=P("groups", None, "tile", None),
        check_vma=False,
    )
```

time: 54 us -> 23.8 us (0.44)
  the two profiles are of different devices: /device:TPU:5 before, /device:TPU:0 now
where the time goes in v1:
time: 23.8 us; the launch traced here: 23.4 us
  starting transfers between devices  7.39 us (31%)
  Pallas kernels  6.41 us (27%)
  local copies, waits for them, and re-layouts  4.59 us (19%)
  waiting for transfers between devices  4.26 us (18%)
  other arithmetic  0.73 us (3%)
    all_to_all x1, starting transfers between devices, per_device(): received = lax.all_to_all(windows, 'tile', 0, 0, tiled=True)  7.39 us
    all_to_all x1, waiting for transfers between devices, per_device(): received = lax.all_to_all(windows, 'tile', 0, 0, tiled=True)  4.26 us
    unnamed x8, local copies, waits for them, and re-layouts  3.94 us
    pallas_call x1, Pallas kernels, per_device(): pl.pallas_call(decode_kernel, out_shape=jax.ShapeDtypeStruct((2 * LT * fr...  2.43 us
    pallas_call x1, Pallas kernels, per_device(): pl.pallas_call(functools.partial(select_kernel, tiles), out_shape=(jax.Sh...  2.28 us
    pallas_call x1, Pallas kernels, per_device(): pl.pallas_call(functools.partial(windows_kernel, tiles), out_shape=jax.Sh...  1.69 us
    mul x1, other arithmetic, per_device(): line_order[:, None] * 8 + jnp.arange(span, dtype=jnp.int32)[None, :]  0.66 us
    add x1, local copies, waits for them, and re-layouts, per_device(): line_order[:, None] * 8 + jnp.arange(span, dtype=jnp.int32)[None, :]  0.65 us
  transfers between devices with their start and end apart: 1, of which 1 were waited for; matrix products, arithmetic and copies ran while one was open for 6% of the time, Pallas kernels for 10%

profile of v1, /device:TPU:0, one launch (start us, length us, event | category | flops | bytes accessed | tf_op | source)
XLA Modules:
  0.0 23.4 jit_solution(5520537529806258056)
XLA Ops:
  0.0 1.7 %shard_map.64 = bf16[256,256]{1,0:T(8,128)(2,1)} custom-call(bf16[128,256]{1,0:T(8,128)(2,1)} %x_ref.1), custom_call_target="tpu_custom_call" | custom-call | tf_op jit(solution)/shard_map/pallas_call | solution.py:132
  1.7 7.4 %all-to-all-start = ((bf16[16,16,256]{2,1,0:T(8,128)(2,1)}), bf16[16,16,256]{2,1,0:T(8,128)(2,1)S(1)}, u32[]{:S(2)}, u32[]{:S(2)}) async-start(bf16[16,16,256]{2,1,0:T(8,128)(2,1)} %bitcast.9), calls=%async_computation | async-start | bytes 262144 | tf_op jit(solution)/shard_map/all_to_all | solution.py:138
  9.1 0.7 %broadcast_multiply_fusion = s32[64]{0:T(128)S(1)} fusion(s32[64]{0:T(128)} %param.7), kind=kLoop, calls=%fused_computation.1 | loop fusion | flops 64 | bytes 512 | tf_op jit(solution)/shard_map/mul | solution.py:139
  9.8 0.1 iota_add_fusion
  9.8 0.7 %add.26.key_ref = s32[1,256]{1,0:T(1,128)} reshape(s32[64,4]{1,0:T(8,128)S(1)} %iota_add_fusion) | data formatting | bytes 2048 | tf_op jit(solution)/shard_map/add | solution.py:139
  10.5 2.3 %shard_map.65 = (bf16[3,512,256]{2,1,0:T(8,128)(2,1)}, f32[8,128]{1,0:T(8,128)}) custom-call(s32[1,256]{1,0:T(1,128)} %add.26.key_ref, s32[16]{0:T(128)} %ids_ref.1, f32[4,8]{1,0:T(4,128)} %table_ref.1, s32[1]{0:T(128)} %bitcast.2.at_ref), custom_call_target="tpu_custom_call" | custom-call | tf_op jit(solution)/shard_map/pallas_call | solution.py:141
  12.8 4.3 %all-to-all-done = bf16[16,16,256]{2,1,0:T(8,128)(2,1)S(1)} async-done(((bf16[16,16,256]{2,1,0:T(8,128)(2,1)}), bf16[16,16,256]{2,1,0:T(8,128)(2,1)S(1)}, u32[]{:S(2)}, u32[]{:S(2)}) %all-to-all-start) | async-done | bytes 131104 | tf_op jit(solution)/shard_map/all_to_all | solution.py:138
  17.0 0.0 copy-start
  17.0 1.5 %copy-done = bf16[3,3,3,256,128]{4,3,2,1,0:T(8,128)(2,1)S(1)} copy-done((bf16[3,3,3,256,128]{4,3,2,1,0:T(8,128)(2,1)S(1)}, bf16[3,3,3,256,128]{4,3,2,1,0:T(8,128)(2,1)}, u32[]{:S(2)}) %copy-start) | copy-done | bytes 1769496
  18.5 0.0 copy-start.1
  18.5 1.1 %copy-done.1 = bf16[3,512,256]{2,1,0:T(8,128)(2,1)S(1)} copy-done((bf16[3,512,256]{2,1,0:T(8,128)(2,1)S(1)}, bf16[3,512,256]{2,1,0:T(8,128)(2,1)}, u32[]{:S(2)}) %copy-start.1) | copy-done | bytes 786456
  19.6 0.0 copy-start.2
  19.6 0.7 %copy-done.2 = f32[8,128]{1,0:T(8,128)S(1)} copy-done((f32[8,128]{1,0:T(8,128)S(1)}, f32[8,128]{1,0:T(8,128)}, u32[]{:S(2)}) %copy-start.2) | copy-done | bytes 4120
  20.3 0.0 copy-start.3
  20.3 0.7 %copy-done.3 = f32[128]{0:T(128)S(1)} copy-done((f32[128]{0:T(128)S(1)}, f32[128]{0:T(128)}, u32[]{:S(2)}) %copy-start.3) | copy-done | bytes 536
  21.0 2.4 %shard_map.66 = bf16[1024,128]{1,0:T(8,128)(2,1)} custom-call(bf16[256,256]{1,0:T(8,128)(2,1)S(1)} %bitcast.7, bf16[3,512,256]{2,1,0:T(8,128)(2,1)S(1)} %copy-done.1, bf16[6912,128]{1,0:T(8,128)(2,1)S(1)} %bitcast.6, f32[1,128]{1,0:T(1,128)S(1)} %bitcast.8, f32[8,128]{1,0:T(8,128)S(1)} %copy-done.2), custom_call_target="tpu_custom_call" | custom-call | tf_op jit(solution)/shard_map/pallas_call | solution.py:151
Async XLA Ops:
  1.7 15.3 %all-to-all-start = ((bf16[16,16,256]{2,1,0:T(8,128)(2,1)}), bf16[16,16,256]{2,1,0:T(8,128)(2,1)S(1)}, u32[]{:S(2)}, u32[]{:S(2)}) async-start(bf16[16,16,256]{2,1,0:T(8,128)(2,1)} %bitcast.9), calls=%async_computation | async-start | bytes 262144 | tf_op jit(solution)/shard_map/all_to_all | solution.py:138
  17.0 1.5 %copy-start = (bf16[3,3,3,256,128]{4,3,2,1,0:T(8,128)(2,1)S(1)}, bf16[3,3,3,256,128]{4,3,2,1,0:T(8,128)(2,1)}, u32[]{:S(2)}) copy-start(bf16[3,3,3,256,128]{4,3,2,1,0:T(8,128)(2,1)} %param.8) | copy-start | bytes 5308420
  18.5 1.1 %copy-start.1 = (bf16[3,512,256]{2,1,0:T(8,128)(2,1)S(1)}, bf16[3,512,256]{2,1,0:T(8,128)(2,1)}, u32[]{:S(2)}) copy-start(bf16[3,512,256]{2,1,0:T(8,128)(2,1)} %get-tuple-element.7.hot_ref) | copy-start | bytes 2359300
  19.6 0.7 %copy-start.2 = (f32[8,128]{1,0:T(8,128)S(1)}, f32[8,128]{1,0:T(8,128)}, u32[]{:S(2)}) copy-start(f32[8,128]{1,0:T(8,128)} %get-tuple-element.8.mix_ref) | copy-start | bytes 12292
  20.3 0.7 %copy-start.3 = (f32[128]{0:T(128)S(1)}, f32[128]{0:T(128)}, u32[]{:S(2)}) copy-start(f32[128]{0:T(128)} %param.9) | copy-start | bytes 1540

commit v2 on v1

--- a/solution.py
+++ b/solution.py
@@ -26,28 +26,43 @@
     return jnp.dot(a, b, preferred_element_type=jnp.float32)
 
 
-def windows_kernel(tiles, x_ref, out_ref):
+def windows_kernel(tiles, x_hbm, out_ref, x_ref, sem):
+    copy = pltpu.make_async_copy(x_hbm, x_ref, sem)
+    copy.start()
     rows_in, _ = x_ref.shape
     rows_out = out_ref.shape[0]
     width = tiles * WD
-    lines = rows_in // width
-    row = lax.broadcasted_iota(jnp.int32, (rows_out, rows_in), 0)
+    span = WD + 2
+    per_tile = rows_in // width * span
+    row = lax.broadcasted_iota(jnp.int32, (rows_out, 1), 0)
+    tile = lax.div(row, per_tile)
+    line = lax.div(lax.rem(row, per_tile), span)
+    at = tile * WD - 1 + lax.rem(row, span)
+    want = jnp.where((at >= 0) & (at < width), line * width + at, -1)
     col = lax.broadcasted_iota(jnp.int32, (rows_out, rows_in), 1)
+    hot = (want == col).astype(jnp.bfloat16)
+    copy.wait()
+    out_ref[...] = dot(hot, x_ref[...]).astype(jnp.bfloat16)
+
+
+def select_kernel(tiles, order_ref, ids_ref, table_ref, at_ref, w_hbm, bias_in, hot_ref, mix_ref, w_ref, bias_ref, sem):
+    copy = pltpu.make_async_copy(w_hbm, w_ref, sem)
+    copy.start()
+    bias_ref[...] = bias_in[...]
+    rows, cols = hot_ref.shape[1:]
+    lines = order_ref.shape[1]
     span = WD + 2
-    tile = row // (lines * span)
-    line = (row // span) % lines
-    at = tile * WD - 1 + row % span
-    hit = (at >= 0) & (at < width) & (line * width + at == col)
-    out_ref[...] = dot(hit.astype(jnp.bfloat16), x_ref[...]).astype(jnp.bfloat16)
-
-
-def select_kernel(tiles, key_ref, ids_ref, table_ref, at_ref, hot_ref, mix_ref):
-    rows, cols = hot_ref.shape[1:]
+    spread = lax.broadcasted_iota(jnp.int32, (lines, cols), 0) == lax.div(
+        lax.broadcasted_iota(jnp.int32, (lines, cols), 1), span
+    )
+    order = jnp.broadcast_to(order_ref[...].astype(jnp.float32), (8, lines))
+    order = jnp.dot(order, spread.astype(jnp.float32), precision=lax.Precision.HIGHEST)[:1]
+    column = lax.rem(lax.broadcasted_iota(jnp.int32, (1, cols), 1), span)
+    key = jnp.broadcast_to(order.astype(jnp.int32) * 8 + column, (rows, cols))
     slot = lax.broadcasted_iota(jnp.int32, (rows, 1), 0)
-    key = jnp.broadcast_to(key_ref[...], (rows, cols))
-    values = NEIGHBOUR, OWN
+    inside = lax.rem(slot, 8)
     for kw in range(3):
-        want = (slot // 8) * 8 + pick(slot % 8, values[0][kw] + values[1][kw])
+        want = slot - inside + pick(inside, NEIGHBOUR[kw] + OWN[kw])
         hot_ref[kw] = (key == want).astype(jnp.bfloat16)
     at = at_ref[0]
     own = ids_ref[at]
@@ -65,8 +80,9 @@
     for q in range(4):
         weight = jnp.where(sub == q, neighbour[q], weight)
         weight = jnp.where(sub == q + 4, mine[q], weight)
-        total = jnp.where(sub % 4 == q, neighbour[q] + mine[q], total)
+        total = jnp.where(lax.rem(sub, 4) == q, neighbour[q] + mine[q], total)
     mix_ref[...] = weight / total
+    copy.wait()
 
 
 def decode_kernel(rows_ref, hot_ref, w_ref, bias_ref, mix_ref, out_ref, lhs_ref, part_ref):
@@ -123,30 +139,42 @@
     return pl.BlockSpec(memory_space=pltpu.SMEM)
 
 
+def hbm():
+    return pl.BlockSpec(memory_space=pl.ANY)
+
+
+def held(value):
+    return pltpu.with_memory_space_constraint(value, pltpu.VMEM)
+
+
 def per_device(latent_rows, line_order, conv_weight, conv_bias, blend_table, blend_ids):
     tiles = lax.axis_size("tile")
     rows, depth = latent_rows.shape
     co = conv_weight.shape[-1]
     lines = line_order.shape[0]
     span = WD + 2
+    weights = conv_weight.reshape(-1, co)
     windows = pl.pallas_call(
         functools.partial(windows_kernel, tiles),
-        out_shape=jax.ShapeDtypeStruct((lines * span, depth), jnp.bfloat16),
-        in_specs=[vmem()],
+        out_shape=pltpu.VMEM((lines * span, depth), jnp.bfloat16),
+        in_specs=[hbm()],
         out_specs=vmem(),
+        scratch_shapes=[pltpu.VMEM((rows, depth), jnp.bfloat16), pltpu.SemaphoreType.DMA],
     )(latent_rows)
     received = lax.all_to_all(windows, "tile", 0, 0, tiled=True)
-    key = (line_order[:, None] * 8 + jnp.arange(span, dtype=jnp.int32)[None, :]).reshape(1, lines * span)
     position = lax.axis_index("tile").astype(jnp.int32).reshape(1)
-    hot, mix = pl.pallas_call(
+    hot, mix, weights, bias = pl.pallas_call(
         functools.partial(select_kernel, tiles),
         out_shape=(
-            jax.ShapeDtypeStruct((3, lines * 8, lines * span), jnp.bfloat16),
-            jax.ShapeDtypeStruct((8, co), jnp.float32),
+            pltpu.VMEM((3, lines * 8, lines * span), jnp.bfloat16),
+            pltpu.VMEM((8, co), jnp.float32),
+            pltpu.VMEM(weights.shape, weights.dtype),
+            pltpu.VMEM((1, co), jnp.float32),
         ),
-        in_specs=[vmem(), smem(), smem(), smem()],
-        out_specs=(vmem(), vmem()),
-    )(key, blend_ids, blend_table, position)
+        in_specs=[vmem(), smem(), smem(), smem(), hbm(), vmem()],
+        out_specs=(vmem(),) * 4,
+        scratch_shapes=[pltpu.SemaphoreType.DMA],
+    )(line_order.reshape(1, -1), blend_ids, blend_table, position, weights, conv_bias.reshape(1, co))
     frame = lines // LT * 8
     out = pl.pallas_call(
         decode_kernel,
@@ -158,7 +186,7 @@
             pltpu.VMEM((9, lines * 8, co), jnp.float32),
         ],
         compiler_params=pltpu.CompilerParams(vmem_limit_bytes=48 * 1024 * 1024),
-    )(received, hot, conv_weight.reshape(-1, co), conv_bias.reshape(1, co), mix)
+    )(held(received), held(hot), held(weights), held(bias), held(mix))
     return out.reshape(2 * LT, lines // LT * 2, 2 * WD, co)
 
 

time: 23.8 us -> 19.8 us (0.83)
  local copies, waits for them, and re-layouts: 4.59 us -> 0 us
  waiting for transfers between devices: 4.26 us -> 5.58 us
  other arithmetic: 0.73 us -> 0 us
    unnamed x8 -> x0, local copies, waits for them, and re-layouts: 3.94 us -> none
    all_to_all x1, waiting for transfers between devices: 4.26 us -> 5.58 us  [per_device(): received = lax.all_to_all(windows, 'tile', 0, 0, tiled=True)]
    mul x1 -> x0, other arithmetic: 0.66 us -> none  [per_device(): line_order[:, None] * 8 + jnp.arange(span, dtype=jnp.int32)[None, :]]
    add x1 -> x0, local copies, waits for them, and re-layouts: 0.65 us -> none  [per_device(): line_order[:, None] * 8 + jnp.arange(span, dtype=jnp.int32)[None, :]]
  transfers between devices with their start and end apart: 1 -> 1, of which waited for: 1 -> 1; matrix products, arithmetic and copies ran while one was open for 6% -> 0% of each run, Pallas kernels for 10% -> 12%
where the time goes in v2:
time: 19.8 us; the launch traced here: 19.5 us
  starting transfers between devices  7.4 us (37%)
  Pallas kernels  6.47 us (33%)
  waiting for transfers between devices  5.58 us (28%)
    all_to_all x1, starting transfers between devices, per_device(): received = lax.all_to_all(windows, 'tile', 0, 0, tiled=True)  7.4 us
    all_to_all x1, waiting for transfers between devices, per_device(): received = lax.all_to_all(windows, 'tile', 0, 0, tiled=True)  5.58 us
    pallas_call x1, Pallas kernels, per_device(): pl.pallas_call(decode_kernel, out_shape=jax.ShapeDtypeStruct((2 * LT * fr...  2.45 us
    pallas_call x1, Pallas kernels, per_device(): pl.pallas_call(functools.partial(select_kernel, tiles), out_shape=(pltpu....  2.34 us
    pallas_call x1, Pallas kernels, per_device(): pl.pallas_call(functools.partial(windows_kernel, tiles), out_shape=pltpu....  1.68 us
  transfers between devices with their start and end apart: 1, of which 1 were waited for; matrix products, arithmetic and copies ran while one was open for 0% of the time, Pallas kernels for 12%

profile of v2, /device:TPU:0, one launch (start us, length us, event | category | flops | bytes accessed | tf_op | source)
XLA Modules:
  0.0 19.5 jit_solution(744722258444612900)
XLA Ops:
  0.0 1.7 %shard_map.64 = bf16[256,256]{1,0:T(8,128)(2,1)} custom-call(bf16[128,256]{1,0:T(8,128)(2,1)} %x_hbm.1), custom_call_target="tpu_custom_call" | custom-call | tf_op jit(solution)/shard_map/pallas_call | solution.py:157
  1.7 7.4 %all-to-all-start = ((bf16[16,16,256]{2,1,0:T(8,128)(2,1)}), bf16[16,16,256]{2,1,0:T(8,128)(2,1)S(1)}, u32[]{:S(2)}, u32[]{:S(2)}) async-start(bf16[16,16,256]{2,1,0:T(8,128)(2,1)} %bitcast), calls=%async_computation | async-start | bytes 262144 | tf_op jit(solution)/shard_map/all_to_all | solution.py:164
  9.1 2.3 %shard_map.65 = (bf16[3,512,256]{2,1,0:T(8,128)(2,1)S(1)}, f32[8,128]{1,0:T(8,128)S(1)}, bf16[6912,128]{1,0:T(8,128)(2,1)S(1)}, f32[1,128]{1,0:T(1,128)S(1)}) custom-call(s32[1,64]{1,0:T(1,128)} %bitcast.9, s32[16]{0:T(128)} %ids_ref.1, f32[4,8]{1,0:T(4,128)} %table_ref.1, s32[1]{0:T(128)} %bitcast.3.at_ref, bf16[6912,128]{1,0:T(8,128)(2,1)} %bitcast.8, ...), custom_call_target="tpu_custom_call" | custom-call | tf_op jit(solution)/shard_map/pallas_call | solution.py:166
  11.4 5.6 %all-to-all-done = bf16[16,16,256]{2,1,0:T(8,128)(2,1)S(1)} async-done(((bf16[16,16,256]{2,1,0:T(8,128)(2,1)}), bf16[16,16,256]{2,1,0:T(8,128)(2,1)S(1)}, u32[]{:S(2)}, u32[]{:S(2)}) %all-to-all-start) | async-done | bytes 131104 | tf_op jit(solution)/shard_map/all_to_all | solution.py:164
  17.0 2.4 %shard_map.66 = bf16[1024,128]{1,0:T(8,128)(2,1)} custom-call(bf16[256,256]{1,0:T(8,128)(2,1)S(1)} %bitcast.7, bf16[3,512,256]{2,1,0:T(8,128)(2,1)S(1)} %get-tuple-element.9.hot_ref, bf16[6912,128]{1,0:T(8,128)(2,1)S(1)} %get-tuple-element.10.w_ref, f32[1,128]{1,0:T(1,128)S(1)} %get-tuple-element.11.bias_ref, f32[8,128]{1,0:T(8,128)S(1)} %get-tuple-element.12.mix_ref), custom_call_target="tpu_custom_call" | custom-call | tf_op jit(solution)/shard_map/pallas_call | solution.py:179
Async XLA Ops:
  1.7 15.3 %all-to-all-start = ((bf16[16,16,256]{2,1,0:T(8,128)(2,1)}), bf16[16,16,256]{2,1,0:T(8,128)(2,1)S(1)}, u32[]{:S(2)}, u32[]{:S(2)}) async-start(bf16[16,16,256]{2,1,0:T(8,128)(2,1)} %bitcast), calls=%async_computation | async-start | bytes 262144 | tf_op jit(solution)/shard_map/all_to_all | solution.py:164

commit v3 on v2

--- a/solution.py
+++ b/solution.py
@@ -12,6 +12,10 @@
 NEIGHBOUR = ((0, 1, None, 2), (1, 1, 2, 2), (1, None, 2, 3))
 OWN = ((0, 1, 1, 2), (1, 1, 2, 2), (1, 2, 2, 3))
 NONE = 7
+
+
+def tile_of(place, tiles):
+    return (tiles + 3 * tiles // 4 - 1 - place) % tiles
 
 
 def pick(index, values):
@@ -35,7 +39,7 @@
     span = WD + 2
     per_tile = rows_in // width * span
     row = lax.broadcasted_iota(jnp.int32, (rows_out, 1), 0)
-    tile = lax.div(row, per_tile)
+    tile = tile_of(lax.div(row, per_tile), tiles)
     line = lax.div(lax.rem(row, per_tile), span)
     at = tile * WD - 1 + lax.rem(row, span)
     want = jnp.where((at >= 0) & (at < width), line * width + at, -1)
@@ -52,9 +56,10 @@
     rows, cols = hot_ref.shape[1:]
     lines = order_ref.shape[1]
     span = WD + 2
-    spread = lax.broadcasted_iota(jnp.int32, (lines, cols), 0) == lax.div(
-        lax.broadcasted_iota(jnp.int32, (lines, cols), 1), span
-    )
+    line_at = lax.div(lax.broadcasted_iota(jnp.int32, (lines, cols), 1), span)
+    per_tile = lines // tiles
+    line_at = tile_of(lax.div(line_at, per_tile), tiles) * per_tile + lax.rem(line_at, per_tile)
+    spread = lax.broadcasted_iota(jnp.int32, (lines, cols), 0) == line_at
     order = jnp.broadcast_to(order_ref[...].astype(jnp.float32), (8, lines))
     order = jnp.dot(order, spread.astype(jnp.float32), precision=lax.Precision.HIGHEST)[:1]
     column = lax.rem(lax.broadcasted_iota(jnp.int32, (1, cols), 1), span)
@@ -161,7 +166,8 @@
         out_specs=vmem(),
         scratch_shapes=[pltpu.VMEM((rows, depth), jnp.bfloat16), pltpu.SemaphoreType.DMA],
     )(latent_rows)
-    received = lax.all_to_all(windows, "tile", 0, 0, tiled=True)
+    order = [tile_of(place, tiles) for place in range(tiles)]
+    received = lax.all_to_all(windows, "tile", 0, 0, axis_index_groups=[order], tiled=True)
     position = lax.axis_index("tile").astype(jnp.int32).reshape(1)
     hot, mix, weights, bias = pl.pallas_call(
         functools.partial(select_kernel, tiles),

time: 19.8 us -> 16.4 us (0.83)
  waiting for transfers between devices: 5.58 us -> 1.85 us
  starting transfers between devices: 7.4 us -> 7.84 us
    all_to_all x1, waiting for transfers between devices: 5.58 us -> 1.85 us  [per_device(): lax.all_to_all(windows, 'tile', 0, 0, axis_index_groups=[order], tiled=True)]
    all_to_all x1, starting transfers between devices: 7.4 us -> 7.84 us  [per_device(): lax.all_to_all(windows, 'tile', 0, 0, axis_index_groups=[order], tiled=True)]
  transfers between devices with their start and end apart: 1 -> 1, of which waited for: 1 -> 1; matrix products, arithmetic and copies ran while one was open for 0% -> 0% of each run, Pallas kernels for 12% -> 14%
where the time goes in v3:
time: 16.4 us; the launch traced here: 16.2 us
  starting transfers between devices  7.84 us (48%)
  Pallas kernels  6.45 us (39%)
  waiting for transfers between devices  1.85 us (11%)
    all_to_all x1, starting transfers between devices, per_device(): lax.all_to_all(windows, 'tile', 0, 0, axis_index_groups=[order], tiled=True)  7.84 us
    pallas_call x1, Pallas kernels, per_device(): pl.pallas_call(decode_kernel, out_shape=jax.ShapeDtypeStruct((2 * LT * fr...  2.45 us
    pallas_call x1, Pallas kernels, per_device(): pl.pallas_call(functools.partial(select_kernel, tiles), out_shape=(pltpu....  2.33 us
    all_to_all x1, waiting for transfers between devices, per_device(): lax.all_to_all(windows, 'tile', 0, 0, axis_index_groups=[order], tiled=True)  1.85 us
    pallas_call x1, Pallas kernels, per_device(): pl.pallas_call(functools.partial(windows_kernel, tiles), out_shape=pltpu....  1.68 us
  transfers between devices with their start and end apart: 1, of which 1 were waited for; matrix products, arithmetic and copies ran while one was open for 0% of the time, Pallas kernels for 14%

profile of v3, /device:TPU:0, one launch (start us, length us, event | category | flops | bytes accessed | tf_op | source)
XLA Modules:
  0.0 16.2 jit_solution(10022319953195616415)
XLA Ops:
  0.0 1.7 %shard_map.64 = bf16[256,256]{1,0:T(8,128)(2,1)} custom-call(bf16[128,256]{1,0:T(8,128)(2,1)} %x_hbm.1), custom_call_target="tpu_custom_call" | custom-call | tf_op jit(solution)/shard_map/pallas_call | solution.py:162
  1.7 7.8 %all-to-all-start = ((bf16[16,16,256]{2,1,0:T(8,128)(2,1)}), bf16[16,16,256]{2,1,0:T(8,128)(2,1)S(1)}, u32[]{:S(2)}, u32[]{:S(2)}) async-start(bf16[16,16,256]{2,1,0:T(8,128)(2,1)} %bitcast), calls=%async_computation | async-start | bytes 262144 | tf_op jit(solution)/shard_map/all_to_all | solution.py:170
  9.5 2.3 %shard_map.65 = (bf16[3,512,256]{2,1,0:T(8,128)(2,1)S(1)}, f32[8,128]{1,0:T(8,128)S(1)}, bf16[6912,128]{1,0:T(8,128)(2,1)S(1)}, f32[1,128]{1,0:T(1,128)S(1)}) custom-call(s32[1,64]{1,0:T(1,128)} %bitcast.9, s32[16]{0:T(128)} %ids_ref.1, f32[4,8]{1,0:T(4,128)} %table_ref.1, s32[1]{0:T(128)} %bitcast.3.at_ref, bf16[6912,128]{1,0:T(8,128)(2,1)} %bitcast.8, ...), custom_call_target="tpu_custom_call" | custom-call | tf_op jit(solution)/shard_map/pallas_call | solution.py:172
  11.9 1.8 %all-to-all-done = bf16[16,16,256]{2,1,0:T(8,128)(2,1)S(1)} async-done(((bf16[16,16,256]{2,1,0:T(8,128)(2,1)}), bf16[16,16,256]{2,1,0:T(8,128)(2,1)S(1)}, u32[]{:S(2)}, u32[]{:S(2)}) %all-to-all-start) | async-done | bytes 131104 | tf_op jit(solution)/shard_map/all_to_all | solution.py:170
  13.7 2.4 %shard_map.66 = bf16[1024,128]{1,0:T(8,128)(2,1)} custom-call(bf16[256,256]{1,0:T(8,128)(2,1)S(1)} %bitcast.7, bf16[3,512,256]{2,1,0:T(8,128)(2,1)S(1)} %get-tuple-element.9.hot_ref, bf16[6912,128]{1,0:T(8,128)(2,1)S(1)} %get-tuple-element.10.w_ref, f32[1,128]{1,0:T(1,128)S(1)} %get-tuple-element.11.bias_ref, f32[8,128]{1,0:T(8,128)S(1)} %get-tuple-element.12.mix_ref), custom_call_target="tpu_custom_call" | custom-call | tf_op jit(solution)/shard_map/pallas_call | solution.py:185
Async XLA Ops:
  1.7 12.0 %all-to-all-start = ((bf16[16,16,256]{2,1,0:T(8,128)(2,1)}), bf16[16,16,256]{2,1,0:T(8,128)(2,1)S(1)}, u32[]{:S(2)}, u32[]{:S(2)}) async-start(bf16[16,16,256]{2,1,0:T(8,128)(2,1)} %bitcast), calls=%async_computation | async-start | bytes 262144 | tf_op jit(solution)/shard_map/all_to_all | solution.py:170

commit v4 on v3

v4 whole, which is shorter than its diff:
```python
import functools

import jax
import jax.numpy as jnp
from jax import lax
from jax.experimental import pallas as pl
from jax.experimental.pallas import tpu as pltpu
from jax.sharding import PartitionSpec as P

LT = 4
WD = 2
NEIGHBOUR = ((0, 1, None, 2), (1, 1, 2, 2), (1, None, 2, 3))
OWN = ((0, 1, 1, 2), (1, 1, 2, 2), (1, 2, 2, 3))
NONE = 7


def tile_of(place, tiles):
    return (tiles + 3 * tiles // 4 - 1 - place) % tiles


def pick(index, values):
    out = jnp.full(index.shape, NONE, jnp.int32)
    for at, value in enumerate(values):
        if value is not None:
            out = jnp.where(index == at, value, out)
    return out


def dot(a, b):
    return jnp.dot(a, b, preferred_element_type=jnp.float32)


def windows_hot(tiles, rows_in, rows_out):
    width = tiles * WD
    span = WD + 2
    per_tile = rows_in // width * span
    row = lax.broadcasted_iota(jnp.int32, (rows_out, 1), 0)
    tile = tile_of(lax.div(row, per_tile), tiles)
    line = lax.div(lax.rem(row, per_tile), span)
    at = tile * WD - 1 + lax.rem(row, span)
    want = jnp.where((at >= 0) & (at < width), line * width + at, -1)
    col = lax.broadcasted_iota(jnp.int32, (rows_out, rows_in), 1)
    return (want == col).astype(jnp.bfloat16)


def line_key(tiles, order, cols):
    lines = order.shape[1]
    span = WD + 2
    per_tile = lines // tiles
    line_at = lax.div(lax.broadcasted_iota(jnp.int32, (lines, cols), 1), span)
    line_at = tile_of(lax.div(line_at, per_tile), tiles) * per_tile + lax.rem(line_at, per_tile)
    spread = lax.broadcasted_iota(jnp.int32, (lines, cols), 0) == line_at
    order = jnp.broadcast_to(order.astype(jnp.float32), (8, lines))
    order = jnp.dot(order, spread.astype(jnp.float32), precision=lax.Precision.HIGHEST)[:1]
    column = lax.rem(lax.broadcasted_iota(jnp.int32, (1, cols), 1), span)
    return order.astype(jnp.int32) * 8 + column


def blend_mix(tiles, at, ids_ref, table_ref, shape):
    own = ids_ref[at]
    lower = ids_ref[jnp.maximum(at - 1, 0)]
    upper = ids_ref[jnp.minimum(at + 1, tiles - 1)]
    has_lower = jnp.where(at > 0, 1.0, 0.0)
    has_upper = jnp.where(at < tiles - 1, 1.0, 0.0)
    wide = 2 * WD + 4
    neighbour = [has_lower * table_ref[lower, wide - 2], has_lower * table_ref[lower, wide - 1]]
    neighbour += [has_upper * table_ref[upper, 0], has_upper * table_ref[upper, 1]]
    mine = [table_ref[own, c] for c in range(2, wide - 2)]
    sub = lax.broadcasted_iota(jnp.int32, shape, 0)
    weight = jnp.zeros(shape, jnp.float32)
    total = jnp.ones(shape, jnp.float32)
    for q in range(4):
        weight = jnp.where(sub == q, neighbour[q], weight)
        weight = jnp.where(sub == q + 4, mine[q], weight)
        total = jnp.where(lax.rem(sub, 4) == q, neighbour[q] + mine[q], total)
    return weight / total


def prepare_kernel(
    tiles, x_hbm, order_hbm, ids_hbm, table_hbm, bias_hbm, at_ref,
    x_ref, take_ref, hot_ref, mix_ref, bias_ref, order_ref, ids_ref, table_ref, sems,
):
    moves = [
        (order_hbm, order_ref), (x_hbm, x_ref), (ids_hbm, ids_ref), (table_hbm, table_ref), (bias_hbm, bias_ref),
    ]
    copies = [pltpu.make_async_copy(a, b, sems.at[n]) for n, (a, b) in enumerate(moves)]
    for copy in copies:
        copy.start()
    take_ref[...] = windows_hot(tiles, *take_ref.shape[::-1])
    rows, cols = hot_ref.shape[1:]
    slot = lax.broadcasted_iota(jnp.int32, (rows, 1), 0)
    inside = lax.rem(slot, 8)
    wants = [slot - inside + pick(inside, NEIGHBOUR[kw] + OWN[kw]) for kw in range(3)]
    copies[0].wait()
    key = jnp.broadcast_to(line_key(tiles, order_ref[...], cols), (rows, cols))
    for kw in range(3):
        hot_ref[kw] = (key == wants[kw]).astype(jnp.bfloat16)
    for copy in copies[2:]:
        copy.wait()
    mix_ref[...] = blend_mix(tiles, at_ref[0], ids_ref, table_ref, mix_ref.shape)
    copies[1].wait()


def windows_kernel(x_ref, take_ref, send_ref):
    send_ref[...] = dot(take_ref[...], x_ref[...]).astype(jnp.bfloat16)


def decode_kernel(rows_ref, hot_ref, w_ref, bias_ref, mix_ref, out_hbm, lhs_ref, part_ref, out_ref, sems):
    depth = rows_ref.shape[1]
    count = hot_ref.shape[1]
    frame = count // LT
    co = w_ref.shape[1]
    tap = 3 * depth
    rows = rows_ref[...]
    for kw in range(3):
        lhs_ref[:, kw * depth:(kw + 1) * depth] = dot(hot_ref[kw], rows).astype(jnp.bfloat16)
    def weights(k):
        return w_ref[k * tap:(k + 1) * tap, :]

    bias = bias_ref[...]
    mix = jnp.concatenate([mix_ref[...]] * (frame // 8), axis=0)
    low = lax.broadcasted_iota(jnp.int32, (frame, co), 0) % 8 < 4
    zero = jnp.zeros((8, co), jnp.float32)
    before = None
    copies = []
    group = count // 4
    for t in range(LT):
        if t * frame % group == 0:
            here = slice(t * frame, t * frame + group)
            lhs = lhs_ref[here, :]
            for k in range(0, 9, 2):
                if k + 1 < 9:
                    both = dot(lhs, jnp.concatenate([weights(k), weights(k + 1)], axis=1))
                    part_ref[k, here] = both[:, :co]
                    part_ref[k + 1, here] = both[:, co:]
                else:
                    part_ref[k, here] = dot(lhs, weights(k))
        now = []
        for kt in range(3):
            p0, p1, p2 = (part_ref[kt * 3 + kh, t * frame:(t + 1) * frame, :] for kh in range(3))
            even = jnp.concatenate([zero, p0[:-8]], axis=0) + (p1 + p2)
            odd = (p0 + p1) + jnp.concatenate([p2[8:], zero], axis=0)
            now.append((even, odd))
        if before is None:
            before = now
        for tp in range(2):
            blended = []
            for hp in range(2):
                middle = before[1][hp] if tp == 0 else now[1][hp]
                value = before[0][hp] + middle + now[2][hp] + bias
                value = value / (1.0 + jnp.exp(-value))
                blended.append(value * mix)
            straight = jnp.where(low, blended[0], blended[1])
            crossed = jnp.where(low, blended[1], blended[0])
            crossed = pltpu.roll(crossed.reshape(frame // 8, 8, co), 4, 1).reshape(frame, co)
            at = (2 * t + tp) * frame
            out_ref[at:at + frame, :] = (straight + crossed).astype(jnp.bfloat16)
            frames = pl.ds(at, frame)
            copies.append(pltpu.make_async_copy(out_ref.at[frames], out_hbm.at[frames], sems.at[2 * t + tp]))
            copies[-1].start()
        before = now
    for copy in copies:
        copy.wait()


def vmem():
    return pl.BlockSpec(memory_space=pltpu.VMEM)


def smem():
    return pl.BlockSpec(memory_space=pltpu.SMEM)


def hbm():
    return pl.BlockSpec(memory_space=pltpu.HBM)


def outside(value):
    return pltpu.with_memory_space_constraint(value, pltpu.HBM)


def held(value):
    return pltpu.with_memory_space_constraint(value, pltpu.VMEM)


def per_device(latent_rows, line_order, conv_weight, conv_bias, blend_table, blend_ids):
    tiles = lax.axis_size("tile")
    rows, depth = latent_rows.shape
    co = conv_weight.shape[-1]
    lines = line_order.shape[0]
    span = WD + 2
    weights = conv_weight.reshape(-1, co)
    order = [tile_of(place, tiles) for place in range(tiles)]
    position = lax.axis_index("tile").astype(jnp.int32).reshape(1)
    x, take, hot, mix, bias = pl.pallas_call(
        functools.partial(prepare_kernel, tiles),
        out_shape=(
            pltpu.VMEM((rows, depth), jnp.bfloat16),
            pltpu.VMEM((lines * span, rows), jnp.bfloat16),
            pltpu.VMEM((3, lines * 8, lines * span), jnp.bfloat16),
            pltpu.VMEM((8, co), jnp.float32),
            pltpu.VMEM((1, co), jnp.float32),
        ),
        in_specs=[hbm()] * 5 + [smem()],
        out_specs=(vmem(),) * 5,
        scratch_shapes=[
            pltpu.VMEM((1, lines), jnp.int32),
            pltpu.SMEM(blend_ids.shape, jnp.int32),
            pltpu.SMEM(blend_table.shape, jnp.float32),
            pltpu.SemaphoreType.DMA((5,)),
        ],
    )(
        *map(outside, (latent_rows, line_order.reshape(1, -1), blend_ids, blend_table, conv_bias.reshape(1, co))),
        position,
    )
    send = pl.pallas_call(
        windows_kernel,
        out_shape=pltpu.VMEM((lines * span, depth), jnp.bfloat16),
        in_specs=[vmem(), vmem()],
        out_specs=vmem(),
        cost_estimate=pl.CostEstimate(flops=10**10, bytes_accessed=10**7, transcendentals=0),
    )(held(x), held(take))
    received = lax.all_to_all(send, "tile", 0, 0, axis_index_groups=[order], tiled=True)
    frame = lines // LT * 8
    out = pl.pallas_call(
        decode_kernel,
        out_shape=jax.ShapeDtypeStruct((2 * LT * frame, co), jnp.bfloat16),
        in_specs=[vmem()] * 5,
        out_specs=hbm(),
        scratch_shapes=[
            pltpu.VMEM((lines * 8, 3 * depth), jnp.bfloat16),
            pltpu.VMEM((9, lines * 8, co), jnp.float32),
            pltpu.VMEM((2 * LT * frame, co), jnp.bfloat16),
            pltpu.SemaphoreType.DMA((2 * LT,)),
        ],
        compiler_params=pltpu.CompilerParams(vmem_limit_bytes=48 * 1024 * 1024),
    )(held(received), held(hot), weights, held(bias), held(mix))
    return out.reshape(2 * LT, lines // LT * 2, 2 * WD, co)


def solution(mesh):
    return jax.shard_map(
        per_device,
        mesh=mesh,
        in_specs=(P(("groups", "tile"), None), P("groups"), P(), P(), P(), P("groups")),
        out_specs=P("groups", None, "tile", None),
        check_vma=False,
    )
```

time: 16.4 us -> 15.4 us (0.939)
  blocking collectives: 0 us -> 11.7 us
  starting transfers between devices: 7.84 us -> 0 us
  Pallas kernels: 6.45 us -> 3.5 us
  waiting for transfers between devices: 1.85 us -> 0 us
    all_to_all x0 -> x1, blocking collectives: none -> 11.7 us  [per_device(): lax.all_to_all(send, 'tile', 0, 0, axis_index_groups=[order], tiled=True)]
    all_to_all x1 -> x0, starting transfers between devices: 7.84 us -> none  [per_device(): lax.all_to_all(windows, 'tile', 0, 0, axis_index_groups=[order], tiled=True)]
    pallas_call x2, Pallas kernels: 4.01 us -> 1.22 us  [the longest x1 1.06 us: per_device(): pl.pallas_call(functools.partial(prepare_kernel, tiles), out_shape=(pltpu...]
    all_to_all x1 -> x0, waiting for transfers between devices: 1.85 us -> none  [per_device(): lax.all_to_all(windows, 'tile', 0, 0, axis_index_groups=[order], tiled=True)]
    pallas_call x1, Pallas kernels: 2.45 us -> 2.28 us  [per_device(): pl.pallas_call(decode_kernel, out_shape=jax.ShapeDtypeStruct((2 * LT * fr...]
  transfers between devices with their start and end apart: 1 -> 0, of which waited for: 1 -> 0; matrix products, arithmetic and copies ran while one was open for 0% -> 0% of each run, Pallas kernels for 14% -> 0%
where the time goes in v4:
time: 15.4 us; the launch traced here: 15.2 us
  blocking collectives  11.7 us (76%)
  Pallas kernels  3.5 us (23%)
    all_to_all x1, blocking collectives, per_device(): lax.all_to_all(send, 'tile', 0, 0, axis_index_groups=[order], tiled=True)  11.7 us
    pallas_call x1, Pallas kernels, per_device(): pl.pallas_call(decode_kernel, out_shape=jax.ShapeDtypeStruct((2 * LT * fr...  2.28 us
    pallas_call x1, Pallas kernels, per_device(): pl.pallas_call(functools.partial(prepare_kernel, tiles), out_shape=(pltpu...  1.06 us

profile of v4, /device:TPU:0, one launch (start us, length us, event | category | flops | bytes accessed | tf_op | source)
XLA Modules:
  0.0 15.2 jit_solution(10401672952394815949)
XLA Ops:
  0.0 1.1 %shard_map.64 = (bf16[128,256]{1,0:T(8,128)(2,1)S(1)}, bf16[256,128]{1,0:T(8,128)(2,1)S(1)}, bf16[3,512,256]{2,1,0:T(8,128)(2,1)S(1)}, f32[8,128]{1,0:T(8,128)S(1)}, f32[1,128]{1,0:T(1,128)S(1)}) custom-call(bf16[128,256]{1,0:T(8,128)(2,1)} %x_hbm.1, s32[1,64]{1,0:T(1,128)} %bitcast.10, s32[16]{0:T(128)} %ids_hbm.1, f32[4,8]{1,0:T(4,128)} %table_hbm.1, ...), custom_call_target="tpu_custom_call" | custom-call | tf_op jit(solution)/shard_map/pallas_call | solution.py:195
  1.1 0.0 copy-start
  1.1 0.2 %shard_map.65 = bf16[256,256]{1,0:T(8,128)(2,1)S(1)} custom-call(bf16[128,256]{1,0:T(8,128)(2,1)S(1)} %get-tuple-element.10.x_ref, bf16[256,128]{1,0:T(8,128)(2,1)S(1)} %get-tuple-element.11.take_ref), custom_call_target="tpu_custom_call" | custom-call | flops 10000000000 | bytes 10000000 | tf_op jit(solution)/shard_map/pallas_call | solution.py:216
  1.3 11.7 %all_to_all.11 = bf16[16,16,256]{2,1,0:T(8,128)(2,1)S(1)} all-to-all(bf16[16,16,256]{2,1,0:T(8,128)(2,1)S(1)} %bitcast.9), channel_id=1, replica_groups={{11,10,9,8,7,6,5,4,3,2,1,0,15,14,13,12},{27,26,25,24,23,22,21,20,19,18,..., dimensions={0} | all-to-all | bytes 262144 | tf_op jit(solution)/shard_map/all_to_all | solution.py:223
  13.0 0.0 copy-done
  13.0 2.3 %shard_map.66 = bf16[1024,128]{1,0:T(8,128)(2,1)} custom-call(bf16[256,256]{1,0:T(8,128)(2,1)S(1)} %bitcast.8, bf16[3,512,256]{2,1,0:T(8,128)(2,1)S(1)} %get-tuple-element.12.hot_ref, bf16[6912,128]{1,0:T(8,128)(2,1)S(1)} %bitcast.7, f32[1,128]{1,0:T(1,128)S(1)} %get-tuple-element.13.bias_ref, f32[8,128]{1,0:T(8,128)S(1)} %get-tuple-element.14.mix_ref), custom_call_target="tpu_custom_call" | custom-call | tf_op jit(solution)/shard_map/pallas_call | solution.py:225
Async XLA Ops:
  1.1 11.9 %copy-start = (bf16[3,3,3,256,128]{4,3,2,1,0:T(8,128)(2,1)S(1)}, bf16[3,3,3,256,128]{4,3,2,1,0:T(8,128)(2,1)}, u32[]{:S(2)}) copy-start(bf16[3,3,3,256,128]{4,3,2,1,0:T(8,128)(2,1)} %param.8) | copy-start | bytes 5308420

commit v5 on v4

--- a/solution.py
+++ b/solution.py
@@ -9,9 +9,10 @@
 
 LT = 4
 WD = 2
-NEIGHBOUR = ((0, 1, None, 2), (1, 1, 2, 2), (1, None, 2, 3))
 OWN = ((0, 1, 1, 2), (1, 1, 2, 2), (1, 2, 2, 3))
+NEIGHBOUR = ((None, 1, None, None), (None, 1, 2, None), (None, None, 2, None))
 NONE = 7
+PACKED = ((1, 0, 2), (0, 0, 1), (0, 0, 2), (1, 1, 1), (1, 1, 2), (0, 1, 1), (0, 1, 2), (1, 0, 1))
 
 
 def tile_of(place, tiles):
@@ -66,14 +67,32 @@
     neighbour = [has_lower * table_ref[lower, wide - 2], has_lower * table_ref[lower, wide - 1]]
     neighbour += [has_upper * table_ref[upper, 0], has_upper * table_ref[upper, 1]]
     mine = [table_ref[own, c] for c in range(2, wide - 2)]
-    sub = lax.broadcasted_iota(jnp.int32, shape, 0)
-    weight = jnp.zeros(shape, jnp.float32)
-    total = jnp.ones(shape, jnp.float32)
+    sub = lax.rem(lax.broadcasted_iota(jnp.int32, shape, 0), 4)
+    other = jnp.zeros(shape, jnp.float32)
+    same = jnp.zeros(shape, jnp.float32)
     for q in range(4):
-        weight = jnp.where(sub == q, neighbour[q], weight)
-        weight = jnp.where(sub == q + 4, mine[q], weight)
-        total = jnp.where(lax.rem(sub, 4) == q, neighbour[q] + mine[q], total)
-    return weight / total
+        other = jnp.where(sub == q, neighbour[q], other)
+        same = jnp.where(sub == q, mine[q], same)
+    total = same + other
+    differs = (sub == 1) | (sub == 2)
+    return jnp.where(differs, same, total) / total, jnp.where(differs, other, 0.0) / total
+
+
+def wanted_keys(rows, lines):
+    height = lines // LT
+    half = height // 2
+    row = lax.broadcasted_iota(jnp.int32, (rows, 1), 0)
+    sub = lax.rem(row, 8)
+    group = lax.div(row, 8)
+    packed = LT // 2 * half
+    own = group >= packed
+    group = jnp.where(own, group - packed, group)
+    later, lower, column = (pick(sub, [entry[n] for entry in PACKED]) for n in range(3))
+    frame = lax.div(group, half) + jnp.where(own, 0, later * (LT // 2))
+    at = lax.rem(group, half) + half * jnp.where(own, lax.div(sub, 4), lower)
+    column = jnp.where(own, lax.rem(sub, 4), column)
+    line = (frame * height + at) * 8
+    return [line + jnp.where(own, pick(column, OWN[kw]), pick(column, NEIGHBOUR[kw])) for kw in range(3)]
 
 
 def prepare_kernel(
@@ -88,16 +107,14 @@
         copy.start()
     take_ref[...] = windows_hot(tiles, *take_ref.shape[::-1])
     rows, cols = hot_ref.shape[1:]
-    slot = lax.broadcasted_iota(jnp.int32, (rows, 1), 0)
-    inside = lax.rem(slot, 8)
-    wants = [slot - inside + pick(inside, NEIGHBOUR[kw] + OWN[kw]) for kw in range(3)]
+    wants = wanted_keys(rows, order_ref.shape[1])
     copies[0].wait()
     key = jnp.broadcast_to(line_key(tiles, order_ref[...], cols), (rows, cols))
     for kw in range(3):
         hot_ref[kw] = (key == wants[kw]).astype(jnp.bfloat16)
     for copy in copies[2:]:
         copy.wait()
-    mix_ref[...] = blend_mix(tiles, at_ref[0], ids_ref, table_ref, mix_ref.shape)
+    mix_ref[0], mix_ref[1] = blend_mix(tiles, at_ref[0], ids_ref, table_ref, mix_ref.shape[1:])
     copies[1].wait()
 
 
@@ -105,60 +122,89 @@
     send_ref[...] = dot(take_ref[...], x_ref[...]).astype(jnp.bfloat16)
 
 
-def decode_kernel(rows_ref, hot_ref, w_ref, bias_ref, mix_ref, out_hbm, lhs_ref, part_ref, out_ref, sems):
+def turn(value, by):
+    shape = value.shape
+    return pltpu.roll(value.reshape(shape[0] // 8, 8, shape[1]), by, 1).reshape(shape)
+
+
+def silu(value):
+    return 0.5 * value * (1.0 + jnp.tanh(0.5 * value))
+
+
+def decode_kernel(rows_ref, hot_ref, w_ref, bias_ref, mix_ref, out_hbm, part_ref, out_ref, sems):
     depth = rows_ref.shape[1]
     count = hot_ref.shape[1]
-    frame = count // LT
     co = w_ref.shape[1]
     tap = 3 * depth
+    frame = count // (LT + LT // 2)
+    groups = frame // 8
     rows = rows_ref[...]
-    for kw in range(3):
-        lhs_ref[:, kw * depth:(kw + 1) * depth] = dot(hot_ref[kw], rows).astype(jnp.bfloat16)
-    def weights(k):
-        return w_ref[k * tap:(k + 1) * tap, :]
-
     bias = bias_ref[...]
-    mix = jnp.concatenate([mix_ref[...]] * (frame // 8), axis=0)
-    low = lax.broadcasted_iota(jnp.int32, (frame, co), 0) % 8 < 4
-    zero = jnp.zeros((8, co), jnp.float32)
+    sub = lax.rem(lax.broadcasted_iota(jnp.int32, (frame, co), 0), 8)
+    low = sub < 4
+    upper_own = low[:8]
+    upper_packed = (sub[:8] < 3) | (sub[:8] == 7)
+    earlier = lax.rem(sub, 4)
+    earlier = (earlier == 1) | (earlier == 2)
+    own_weight = jnp.concatenate([mix_ref[0]] * groups, axis=0)
+    other_weight = jnp.concatenate([mix_ref[1]] * groups, axis=0)
+
+    def multiply(at, size):
+        here = slice(at, at + size)
+        lhs = jnp.concatenate([dot(hot_ref[kw, here], rows).astype(jnp.bfloat16) for kw in range(3)], axis=1)
+        for k in range(0, 9, 2):
+            if k + 1 < 9:
+                pair = [w_ref[n * tap:(n + 1) * tap, :] for n in (k, k + 1)]
+                both = dot(lhs, jnp.concatenate(pair, axis=1))
+                part_ref[k, here] = both[:, :co]
+                part_ref[k + 1, here] = both[:, co:]
+            else:
+                part_ref[k, here] = dot(lhs, w_ref[k * tap:(k + 1) * tap, :])
+
+    def over_rows(at, upper):
+        sums = []
+        for kt in range(3):
+            p0, p1, p2 = (part_ref[kt * 3 + kh, at:at + frame, :] for kh in range(3))
+            above = jnp.concatenate([jnp.where(upper, 0.0, turn(p0[-8:], 4)), p0[:-8]], axis=0)
+            below = jnp.concatenate([p2[8:], jnp.where(upper, turn(p2[:8], 4), 0.0)], axis=0)
+            sums.append((above + (p1 + p2), (p0 + p1) + below))
+        return sums
+
+    def decoded(before, now):
+        return [
+            [silu(before[0][hp] + (now if tp else before)[1][hp] + now[2][hp] + bias) for hp in range(2)]
+            for tp in range(2)
+        ]
+
+    first = LT // 2 * frame
+    multiply(0, count * 2 // 3)
+    sums = [over_rows(n * frame, upper_packed) for n in range(LT // 2)]
+    wrapped = [
+        [jnp.where(earlier, sums[0][kt][hp], turn(sums[-1][kt][hp], 6)) for hp in range(2)] for kt in range(2)
+    ]
+    others = [decoded(before, now) for before, now in zip([wrapped] + sums[:-1], sums)]
     before = None
     copies = []
-    group = count // 4
     for t in range(LT):
-        if t * frame % group == 0:
-            here = slice(t * frame, t * frame + group)
-            lhs = lhs_ref[here, :]
-            for k in range(0, 9, 2):
-                if k + 1 < 9:
-                    both = dot(lhs, jnp.concatenate([weights(k), weights(k + 1)], axis=1))
-                    part_ref[k, here] = both[:, :co]
-                    part_ref[k + 1, here] = both[:, co:]
-                else:
-                    part_ref[k, here] = dot(lhs, weights(k))
-        now = []
-        for kt in range(3):
-            p0, p1, p2 = (part_ref[kt * 3 + kh, t * frame:(t + 1) * frame, :] for kh in range(3))
-            even = jnp.concatenate([zero, p0[:-8]], axis=0) + (p1 + p2)
-            odd = (p0 + p1) + jnp.concatenate([p2[8:], zero], axis=0)
-            now.append((even, odd))
-        if before is None:
-            before = now
+        if first + t * frame == count * 2 // 3:
+            multiply(count * 2 // 3, count - count * 2 // 3)
+        now = over_rows(first + t * frame, upper_own)
+        own = decoded(now if before is None else before, now)
+        before = now
         for tp in range(2):
             blended = []
             for hp in range(2):
-                middle = before[1][hp] if tp == 0 else now[1][hp]
-                value = before[0][hp] + middle + now[2][hp] + bias
-                value = value / (1.0 + jnp.exp(-value))
-                blended.append(value * mix)
-            straight = jnp.where(low, blended[0], blended[1])
-            crossed = jnp.where(low, blended[1], blended[0])
-            crossed = pltpu.roll(crossed.reshape(frame // 8, 8, co), 4, 1).reshape(frame, co)
-            at = (2 * t + tp) * frame
-            out_ref[at:at + frame, :] = (straight + crossed).astype(jnp.bfloat16)
-            frames = pl.ds(at, frame)
-            copies.append(pltpu.make_async_copy(out_ref.at[frames], out_hbm.at[frames], sems.at[2 * t + tp]))
-            copies[-1].start()
-        before = now
+                other = others[t % (LT // 2)][tp][hp]
+                if t >= LT // 2:
+                    other = turn(other, 2)
+                blended.append(own[tp][hp] * own_weight + other * other_weight)
+            even, odd = blended
+            at = (2 * t + tp) * 2 * frame
+            out_ref[at:at + frame, :] = jnp.where(low, even, turn(odd, 4)).astype(jnp.bfloat16)
+            out_ref[at + frame:at + 2 * frame, :] = jnp.where(low, turn(even, 4), odd).astype(jnp.bfloat16)
+        both = pl.ds(t * 4 * frame, 4 * frame)
+        copies.append(pltpu.make_async_copy(out_ref.at[both], out_hbm.at[both], sems.at[t]))
+        copies[-1].start()
     for copy in copies:
         copy.wait()
 
@@ -190,6 +236,8 @@
     lines = line_order.shape[0]
     span = WD + 2
     weights = conv_weight.reshape(-1, co)
+    frame = lines // LT * 4
+    count = (LT + LT // 2) * frame
     order = [tile_of(place, tiles) for place in range(tiles)]
     position = lax.axis_index("tile").astype(jnp.int32).reshape(1)
     x, take, hot, mix, bias = pl.pallas_call(
@@ -197,8 +245,8 @@
         out_shape=(
             pltpu.VMEM((rows, depth), jnp.bfloat16),
             pltpu.VMEM((lines * span, rows), jnp.bfloat16),
-            pltpu.VMEM((3, lines * 8, lines * span), jnp.bfloat16),
-            pltpu.VMEM((8, co), jnp.float32),
+            pltpu.VMEM((3, count, lines * span), jnp.bfloat16),
+            pltpu.VMEM((2, 8, co), jnp.float32),
             pltpu.VMEM((1, co), jnp.float32),
         ),
         in_specs=[hbm()] * 5 + [smem()],
@@ -221,17 +269,15 @@
         cost_estimate=pl.CostEstimate(flops=10**10, bytes_accessed=10**7, transcendentals=0),
     )(held(x), held(take))
     received = lax.all_to_all(send, "tile", 0, 0, axis_index_groups=[order], tiled=True)
-    frame = lines // LT * 8
     out = pl.pallas_call(
         decode_kernel,
-        out_shape=jax.ShapeDtypeStruct((2 * LT * frame, co), jnp.bfloat16),
+        out_shape=jax.ShapeDtypeStruct((4 * LT * frame, co), jnp.bfloat16),
         in_specs=[vmem()] * 5,
         out_specs=hbm(),
         scratch_shapes=[
-            pltpu.VMEM((lines * 8, 3 * depth), jnp.bfloat16),
-            pltpu.VMEM((9, lines * 8, co), jnp.float32),
-            pltpu.VMEM((2 * LT * frame, co), jnp.bfloat16),
-            pltpu.SemaphoreType.DMA((2 * LT,)),
+            pltpu.VMEM((9, count, co), jnp.float32),
+            pltpu.VMEM((4 * LT * frame, co), jnp.bfloat16),
+            pltpu.SemaphoreType.DMA((LT,)),
         ],
         compiler_params=pltpu.CompilerParams(vmem_limit_bytes=48 * 1024 * 1024),
     )(held(received), held(hot), weights, held(bias), held(mix))

time: 15.4 us -> 15.2 us (0.987)
  Pallas kernels: 3.5 us -> 3.24 us
    pallas_call x1, Pallas kernels: 2.28 us -> 2.06 us  [per_device(): pl.pallas_call(decode_kernel, out_shape=jax.ShapeDtypeStruct((4 * LT * fr...]
where the time goes in v5:
time: 15.2 us; the launch traced here: 15 us
  blocking collectives  11.7 us (77%)
  Pallas kernels  3.24 us (21%)
    all_to_all x1, blocking collectives, per_device(): lax.all_to_all(send, 'tile', 0, 0, axis_index_groups=[order], tiled=True)  11.7 us
    pallas_call x1, Pallas kernels, per_device(): pl.pallas_call(decode_kernel, out_shape=jax.ShapeDtypeStruct((4 * LT * fr...  2.06 us
    pallas_call x1, Pallas kernels, per_device(): pl.pallas_call(functools.partial(prepare_kernel, tiles), out_shape=(pltpu...  1.01 us

profile of v5, /device:TPU:0, one launch (start us, length us, event | category | flops | bytes accessed | tf_op | source)
XLA Modules:
  0.0 15.0 jit_solution(13381530854640966877)
XLA Ops:
  0.0 1.0 %shard_map.64 = (bf16[128,256]{1,0:T(8,128)(2,1)S(1)}, bf16[256,128]{1,0:T(8,128)(2,1)S(1)}, bf16[3,384,256]{2,1,0:T(8,128)(2,1)S(1)}, f32[2,8,128]{2,1,0:T(8,128)S(1)}, f32[1,128]{1,0:T(1,128)S(1)}) custom-call(bf16[128,256]{1,0:T(8,128)(2,1)} %x_hbm.1, s32[1,64]{1,0:T(1,128)} %bitcast.10, s32[16]{0:T(128)} %ids_hbm.1, f32[4,8]{1,0:T(4,128)} %table_hbm.1, ...), custom_call_target="tpu_custom_call" | custom-call | tf_op jit(solution)/shard_map/pallas_call | solution.py:243
  1.0 0.0 copy-start
  1.0 0.2 %shard_map.65 = bf16[256,256]{1,0:T(8,128)(2,1)S(1)} custom-call(bf16[128,256]{1,0:T(8,128)(2,1)S(1)} %get-tuple-element.10.x_ref, bf16[256,128]{1,0:T(8,128)(2,1)S(1)} %get-tuple-element.11.take_ref), custom_call_target="tpu_custom_call" | custom-call | flops 10000000000 | bytes 10000000 | tf_op jit(solution)/shard_map/pallas_call | solution.py:264
  1.2 11.7 %all_to_all.11 = bf16[16,16,256]{2,1,0:T(8,128)(2,1)S(1)} all-to-all(bf16[16,16,256]{2,1,0:T(8,128)(2,1)S(1)} %bitcast.9), channel_id=1, replica_groups={{11,10,9,8,7,6,5,4,3,2,1,0,15,14,13,12},{27,26,25,24,23,22,21,20,19,18,..., dimensions={0} | all-to-all | bytes 262144 | tf_op jit(solution)/shard_map/all_to_all | solution.py:271
  12.9 0.0 copy-done
  12.9 2.1 %shard_map.66 = bf16[1024,128]{1,0:T(8,128)(2,1)} custom-call(bf16[256,256]{1,0:T(8,128)(2,1)S(1)} %bitcast.8, bf16[3,384,256]{2,1,0:T(8,128)(2,1)S(1)} %get-tuple-element.12.hot_ref, bf16[6912,128]{1,0:T(8,128)(2,1)S(1)} %bitcast.7, f32[1,128]{1,0:T(1,128)S(1)} %get-tuple-element.13.bias_ref, f32[2,8,128]{2,1,0:T(8,128)S(1)} %get-tuple-element.14.mix_ref), custom_call_target="tpu_custom_call" | custom-call | tf_op jit(solution)/shard_map/pallas_call | solution.py:272
Async XLA Ops:
  1.0 11.9 %copy-start = (bf16[3,3,3,256,128]{4,3,2,1,0:T(8,128)(2,1)S(1)}, bf16[3,3,3,256,128]{4,3,2,1,0:T(8,128)(2,1)}, u32[]{:S(2)}) copy-start(bf16[3,3,3,256,128]{4,3,2,1,0:T(8,128)(2,1)} %param.8) | copy-start | bytes 5308420

commit v6 on v5

--- a/solution.py
+++ b/solution.py
@@ -12,11 +12,8 @@
 OWN = ((0, 1, 1, 2), (1, 1, 2, 2), (1, 2, 2, 3))
 NEIGHBOUR = ((None, 1, None, None), (None, 1, 2, None), (None, None, 2, None))
 NONE = 7
+MEASURED = (11, 1, 15, 12, 6, 13, 10, 14, 4, 3, 8, 0, 5, 2, 7, 9)
 PACKED = ((1, 0, 2), (0, 0, 1), (0, 0, 2), (1, 1, 1), (1, 1, 2), (0, 1, 1), (0, 1, 2), (1, 0, 1))
-
-
-def tile_of(place, tiles):
-    return (tiles + 3 * tiles // 4 - 1 - place) % tiles
 
 
 def pick(index, values):
@@ -27,6 +24,12 @@
     return out
 
 
+def order_of(tiles):
+    if tiles == len(MEASURED):
+        return MEASURED
+    return tuple((tiles + 3 * tiles // 4 - 1 - place) % tiles for place in range(tiles))
+
+
 def dot(a, b):
     return jnp.dot(a, b, preferred_element_type=jnp.float32)
 
@@ -36,7 +39,7 @@
     span = WD + 2
     per_tile = rows_in // width * span
     row = lax.broadcasted_iota(jnp.int32, (rows_out, 1), 0)
-    tile = tile_of(lax.div(row, per_tile), tiles)
+    tile = pick(lax.div(row, per_tile), order_of(tiles))
     line = lax.div(lax.rem(row, per_tile), span)
     at = tile * WD - 1 + lax.rem(row, span)
     want = jnp.where((at >= 0) & (at < width), line * width + at, -1)
@@ -48,8 +51,8 @@
     lines = order.shape[1]
     span = WD + 2
     per_tile = lines // tiles
-    line_at = lax.div(lax.broadcasted_iota(jnp.int32, (lines, cols), 1), span)
-    line_at = tile_of(lax.div(line_at, per_tile), tiles) * per_tile + lax.rem(line_at, per_tile)
+    line_at = lax.div(lax.broadcasted_iota(jnp.int32, (1, cols), 1), span)
+    line_at = pick(lax.div(line_at, per_tile), order_of(tiles)) * per_tile + lax.rem(line_at, per_tile)
     spread = lax.broadcasted_iota(jnp.int32, (lines, cols), 0) == line_at
     order = jnp.broadcast_to(order.astype(jnp.float32), (8, lines))
     order = jnp.dot(order, spread.astype(jnp.float32), precision=lax.Precision.HIGHEST)[:1]
@@ -238,7 +241,6 @@
     weights = conv_weight.reshape(-1, co)
     frame = lines // LT * 4
     count = (LT + LT // 2) * frame
-    order = [tile_of(place, tiles) for place in range(tiles)]
     position = lax.axis_index("tile").astype(jnp.int32).reshape(1)
     x, take, hot, mix, bias = pl.pallas_call(
         functools.partial(prepare_kernel, tiles),
@@ -268,7 +270,7 @@
         out_specs=vmem(),
         cost_estimate=pl.CostEstimate(flops=10**10, bytes_accessed=10**7, transcendentals=0),
     )(held(x), held(take))
-    received = lax.all_to_all(send, "tile", 0, 0, axis_index_groups=[order], tiled=True)
+    received = lax.all_to_all(send, "tile", 0, 0, axis_index_groups=[list(order_of(tiles))], tiled=True)
     out = pl.pallas_call(
         decode_kernel,
         out_shape=jax.ShapeDtypeStruct((4 * LT * frame, co), jnp.bfloat16),

time: 15.2 us -> 14.5 us (0.954)
  blocking collectives: 11.7 us -> 11 us
    all_to_all x1, blocking collectives: 11.7 us -> 11 us  [per_device(): lax.all_to_all(send, 'tile', 0, 0, axis_index_groups=[list(order_of(tiles...]
where the time goes in v6:
time: 14.5 us; the launch traced here: 14.3 us
  blocking collectives  11 us (76%)
  Pallas kernels  3.24 us (22%)
    all_to_all x1, blocking collectives, per_device(): lax.all_to_all(send, 'tile', 0, 0, axis_index_groups=[list(order_of(tiles...  11 us
    pallas_call x1, Pallas kernels, per_device(): pl.pallas_call(decode_kernel, out_shape=jax.ShapeDtypeStruct((4 * LT * fr...  2.06 us
    pallas_call x1, Pallas kernels, per_device(): pl.pallas_call(functools.partial(prepare_kernel, tiles), out_shape=(pltpu...  1.01 us

profile of v6, /device:TPU:0, one launch (start us, length us, event | category | flops | bytes accessed | tf_op | source)
XLA Modules:
  0.0 14.3 jit_solution(130848536329206430)
XLA Ops:
  0.0 1.0 %shard_map.64 = (bf16[128,256]{1,0:T(8,128)(2,1)S(1)}, bf16[256,128]{1,0:T(8,128)(2,1)S(1)}, bf16[3,384,256]{2,1,0:T(8,128)(2,1)S(1)}, f32[2,8,128]{2,1,0:T(8,128)S(1)}, f32[1,128]{1,0:T(1,128)S(1)}) custom-call(bf16[128,256]{1,0:T(8,128)(2,1)} %x_hbm.1, s32[1,64]{1,0:T(1,128)} %bitcast.10, s32[16]{0:T(128)} %ids_hbm.1, f32[4,8]{1,0:T(4,128)} %table_hbm.1, ...), custom_call_target="tpu_custom_call" | custom-call | tf_op jit(solution)/shard_map/pallas_call | solution.py:245
  1.0 0.0 copy-start
  1.0 0.2 %shard_map.65 = bf16[256,256]{1,0:T(8,128)(2,1)S(1)} custom-call(bf16[128,256]{1,0:T(8,128)(2,1)S(1)} %get-tuple-element.10.x_ref, bf16[256,128]{1,0:T(8,128)(2,1)S(1)} %get-tuple-element.11.take_ref), custom_call_target="tpu_custom_call" | custom-call | flops 10000000000 | bytes 10000000 | tf_op jit(solution)/shard_map/pallas_call | solution.py:266
  1.2 11.0 %all_to_all.11 = bf16[16,16,256]{2,1,0:T(8,128)(2,1)S(1)} all-to-all(bf16[16,16,256]{2,1,0:T(8,128)(2,1)S(1)} %bitcast.9), channel_id=1, replica_groups={{11,1,15,12,6,13,10,14,4,3,8,0,5,2,7,9},{27,17,31,28,22,29,26,30,20,19,..., dimensions={0} | all-to-all | bytes 262144 | tf_op jit(solution)/shard_map/all_to_all | solution.py:273
  12.2 0.0 copy-done
  12.2 2.1 %shard_map.66 = bf16[1024,128]{1,0:T(8,128)(2,1)} custom-call(bf16[256,256]{1,0:T(8,128)(2,1)S(1)} %bitcast.8, bf16[3,384,256]{2,1,0:T(8,128)(2,1)S(1)} %get-tuple-element.12.hot_ref, bf16[6912,128]{1,0:T(8,128)(2,1)S(1)} %bitcast.7, f32[1,128]{1,0:T(1,128)S(1)} %get-tuple-element.13.bias_ref, f32[2,8,128]{2,1,0:T(8,128)S(1)} %get-tuple-element.14.mix_ref), custom_call_target="tpu_custom_call" | custom-call | tf_op jit(solution)/shard_map/pallas_call | solution.py:274
Async XLA Ops:
  1.0 11.2 %copy-start = (bf16[3,3,3,256,128]{4,3,2,1,0:T(8,128)(2,1)S(1)}, bf16[3,3,3,256,128]{4,3,2,1,0:T(8,128)(2,1)}, u32[]{:S(2)}) copy-start(bf16[3,3,3,256,128]{4,3,2,1,0:T(8,128)(2,1)} %param.8) | copy-start | bytes 5308420

commit v7 on v6

--- a/solution.py
+++ b/solution.py
@@ -9,18 +9,15 @@
 
 LT = 4
 WD = 2
-OWN = ((0, 1, 1, 2), (1, 1, 2, 2), (1, 2, 2, 3))
-NEIGHBOUR = ((None, 1, None, None), (None, 1, 2, None), (None, None, 2, None))
-NONE = 7
+TAKES = ((0, 1, 1, 2), (1, 1, 2, 2), (1, 2, 2, 3))
 MEASURED = (11, 1, 15, 12, 6, 13, 10, 14, 4, 3, 8, 0, 5, 2, 7, 9)
 PACKED = ((1, 0, 2), (0, 0, 1), (0, 0, 2), (1, 1, 1), (1, 1, 2), (0, 1, 1), (0, 1, 2), (1, 0, 1))
 
 
 def pick(index, values):
-    out = jnp.full(index.shape, NONE, jnp.int32)
-    for at, value in enumerate(values):
-        if value is not None:
-            out = jnp.where(index == at, value, out)
+    out = jnp.full(index.shape, values[0], jnp.int32)
+    for at, value in enumerate(values[1:], 1):
+        out = jnp.where(index == at, value, out)
     return out
 
 
@@ -54,8 +51,9 @@
     line_at = lax.div(lax.broadcasted_iota(jnp.int32, (1, cols), 1), span)
     line_at = pick(lax.div(line_at, per_tile), order_of(tiles)) * per_tile + lax.rem(line_at, per_tile)
     spread = lax.broadcasted_iota(jnp.int32, (lines, cols), 0) == line_at
-    order = jnp.broadcast_to(order.astype(jnp.float32), (8, lines))
-    order = jnp.dot(order, spread.astype(jnp.float32), precision=lax.Precision.HIGHEST)[:1]
+    digits = jnp.concatenate([lax.div(order, 128), lax.rem(order, 128)] * 4, axis=0)
+    digits = dot(digits.astype(jnp.float32).astype(jnp.bfloat16), spread.astype(jnp.float32).astype(jnp.bfloat16))
+    order = digits[:1] * 128.0 + digits[1:2]
     column = lax.rem(lax.broadcasted_iota(jnp.int32, (1, cols), 1), span)
     return order.astype(jnp.int32) * 8 + column
 
@@ -87,15 +85,9 @@
     row = lax.broadcasted_iota(jnp.int32, (rows, 1), 0)
     sub = lax.rem(row, 8)
     group = lax.div(row, 8)
-    packed = LT // 2 * half
-    own = group >= packed
-    group = jnp.where(own, group - packed, group)
-    later, lower, column = (pick(sub, [entry[n] for entry in PACKED]) for n in range(3))
-    frame = lax.div(group, half) + jnp.where(own, 0, later * (LT // 2))
-    at = lax.rem(group, half) + half * jnp.where(own, lax.div(sub, 4), lower)
-    column = jnp.where(own, lax.rem(sub, 4), column)
-    line = (frame * height + at) * 8
-    return [line + jnp.where(own, pick(column, OWN[kw]), pick(column, NEIGHBOUR[kw])) for kw in range(3)]
+    at = lax.rem(group, half) + half * lax.div(sub, 4)
+    line = (lax.div(group, half) * height + at) * 8
+    return [line + pick(lax.rem(sub, 4), TAKES[kw]) for kw in range(3)]
 
 
 def prepare_kernel(
@@ -139,37 +131,38 @@
     count = hot_ref.shape[1]
     co = w_ref.shape[1]
     tap = 3 * depth
-    frame = count // (LT + LT // 2)
+    frame = count // LT
     groups = frame // 8
     rows = rows_ref[...]
     bias = bias_ref[...]
     sub = lax.rem(lax.broadcasted_iota(jnp.int32, (frame, co), 0), 8)
     low = sub < 4
-    upper_own = low[:8]
-    upper_packed = (sub[:8] < 3) | (sub[:8] == 7)
-    earlier = lax.rem(sub, 4)
-    earlier = (earlier == 1) | (earlier == 2)
     own_weight = jnp.concatenate([mix_ref[0]] * groups, axis=0)
     other_weight = jnp.concatenate([mix_ref[1]] * groups, axis=0)
 
     def multiply(at, size):
         here = slice(at, at + size)
-        lhs = jnp.concatenate([dot(hot_ref[kw, here], rows).astype(jnp.bfloat16) for kw in range(3)], axis=1)
+        left = [dot(hot_ref[kw, here], rows).astype(jnp.bfloat16) for kw in range(3)]
         for k in range(0, 9, 2):
-            if k + 1 < 9:
-                pair = [w_ref[n * tap:(n + 1) * tap, :] for n in (k, k + 1)]
-                both = dot(lhs, jnp.concatenate(pair, axis=1))
-                part_ref[k, here] = both[:, :co]
-                part_ref[k + 1, here] = both[:, co:]
-            else:
-                part_ref[k, here] = dot(lhs, w_ref[k * tap:(k + 1) * tap, :])
-
-    def over_rows(at, upper):
+            taps = range(k, min(k + 2, 9))
+            r0, r1, r2 = (
+                dot(left[kw], jnp.concatenate([w_ref[n * tap + kw * depth:n * tap + (kw + 1) * depth, :] for n in taps], axis=1))
+                for kw in range(3)
+            )
+            first = lax.rem(lax.broadcasted_iota(jnp.int32, r0.shape, 0), 4) < 2
+            own = r0 + r1 + r2
+            other = r1 + jnp.where(first, r0, r2)
+            for n in taps:
+                lanes = slice((n - k) * co, (n - k + 1) * co)
+                part_ref[0, n, here] = own[:, lanes]
+                part_ref[1, n, here] = other[:, lanes]
+
+    def over_rows(which, at):
         sums = []
         for kt in range(3):
-            p0, p1, p2 = (part_ref[kt * 3 + kh, at:at + frame, :] for kh in range(3))
-            above = jnp.concatenate([jnp.where(upper, 0.0, turn(p0[-8:], 4)), p0[:-8]], axis=0)
-            below = jnp.concatenate([p2[8:], jnp.where(upper, turn(p2[:8], 4), 0.0)], axis=0)
+            p0, p1, p2 = (part_ref[which, kt * 3 + kh, at:at + frame, :] for kh in range(3))
+            above = jnp.concatenate([jnp.where(low[:8], 0.0, turn(p0[-8:], 4)), p0[:-8]], axis=0)
+            below = jnp.concatenate([p2[8:], jnp.where(low[:8], turn(p2[:8], 4), 0.0)], axis=0)
             sums.append((above + (p1 + p2), (p0 + p1) + below))
         return sums
 
@@ -179,28 +172,16 @@
             for tp in range(2)
         ]
 
-    first = LT // 2 * frame
-    multiply(0, count * 2 // 3)
-    sums = [over_rows(n * frame, upper_packed) for n in range(LT // 2)]
-    wrapped = [
-        [jnp.where(earlier, sums[0][kt][hp], turn(sums[-1][kt][hp], 6)) for hp in range(2)] for kt in range(2)
-    ]
-    others = [decoded(before, now) for before, now in zip([wrapped] + sums[:-1], sums)]
     before = None
     copies = []
     for t in range(LT):
-        if first + t * frame == count * 2 // 3:
-            multiply(count * 2 // 3, count - count * 2 // 3)
-        now = over_rows(first + t * frame, upper_own)
-        own = decoded(now if before is None else before, now)
+        if t % 4 == 0:
+            multiply(t * frame, 4 * frame)
+        now = [over_rows(which, t * frame) for which in range(2)]
+        own, other = (decoded(*pair) for pair in zip(now if before is None else before, now))
         before = now
         for tp in range(2):
-            blended = []
-            for hp in range(2):
-                other = others[t % (LT // 2)][tp][hp]
-                if t >= LT // 2:
-                    other = turn(other, 2)
-                blended.append(own[tp][hp] * own_weight + other * other_weight)
+            blended = [own[tp][hp] * own_weight + other[tp][hp] * other_weight for hp in range(2)]
             even, odd = blended
             at = (2 * t + tp) * 2 * frame
             out_ref[at:at + frame, :] = jnp.where(low, even, turn(odd, 4)).astype(jnp.bfloat16)
@@ -240,7 +221,7 @@
     span = WD + 2
     weights = conv_weight.reshape(-1, co)
     frame = lines // LT * 4
-    count = (LT + LT // 2) * frame
+    count = LT * frame
     position = lax.axis_index("tile").astype(jnp.int32).reshape(1)
     x, take, hot, mix, bias = pl.pallas_call(
         functools.partial(prepare_kernel, tiles),
@@ -277,7 +258,7 @@
         in_specs=[vmem()] * 5,
         out_specs=hbm(),
         scratch_shapes=[
-            pltpu.VMEM((9, count, co), jnp.float32),
+            pltpu.VMEM((2, 9, count, co), jnp.float32),
             pltpu.VMEM((4 * LT * frame, co), jnp.bfloat16),
             pltpu.SemaphoreType.DMA((LT,)),
         ],

time: 14.5 us -> 14.1 us (0.972)
  Pallas kernels: 3.24 us -> 2.93 us
    pallas_call x1, Pallas kernels: 2.06 us -> 1.82 us  [per_device(): pl.pallas_call(decode_kernel, out_shape=jax.ShapeDtypeStruct((4 * LT * fr...]
where the time goes in v7:
time: 14.1 us; the launch traced here: 14 us
  blocking collectives  11 us (78%)
  Pallas kernels  2.93 us (21%)
    all_to_all x1, blocking collectives, per_device(): lax.all_to_all(send, 'tile', 0, 0, axis_index_groups=[list(order_of(tiles...  11 us
    pallas_call x1, Pallas kernels, per_device(): pl.pallas_call(decode_kernel, out_shape=jax.ShapeDtypeStruct((4 * LT * fr...  1.82 us
    pallas_call x1, Pallas kernels, per_device(): pl.pallas_call(functools.partial(prepare_kernel, tiles), out_shape=(pltpu...  0.95 us

profile of v7, /device:TPU:0, one launch (start us, length us, event | category | flops | bytes accessed | tf_op | source)
XLA Modules:
  0.0 14.0 jit_solution(9482032438414691081)
XLA Ops:
  0.0 1.0 %shard_map.64 = (bf16[128,256]{1,0:T(8,128)(2,1)S(1)}, bf16[256,128]{1,0:T(8,128)(2,1)S(1)}, bf16[3,256,256]{2,1,0:T(8,128)(2,1)S(1)}, f32[2,8,128]{2,1,0:T(8,128)S(1)}, f32[1,128]{1,0:T(1,128)S(1)}) custom-call(bf16[128,256]{1,0:T(8,128)(2,1)} %x_hbm.1, s32[1,64]{1,0:T(1,128)} %bitcast.10, s32[16]{0:T(128)} %ids_hbm.1, f32[4,8]{1,0:T(4,128)} %table_hbm.1, ...), custom_call_target="tpu_custom_call" | custom-call | tf_op jit(solution)/shard_map/pallas_call | solution.py:226
  1.0 0.0 copy-start
  1.0 0.2 %shard_map.65 = bf16[256,256]{1,0:T(8,128)(2,1)S(1)} custom-call(bf16[128,256]{1,0:T(8,128)(2,1)S(1)} %get-tuple-element.10.x_ref, bf16[256,128]{1,0:T(8,128)(2,1)S(1)} %get-tuple-element.11.take_ref), custom_call_target="tpu_custom_call" | custom-call | flops 10000000000 | bytes 10000000 | tf_op jit(solution)/shard_map/pallas_call | solution.py:247
  1.1 11.0 %all_to_all.11 = bf16[16,16,256]{2,1,0:T(8,128)(2,1)S(1)} all-to-all(bf16[16,16,256]{2,1,0:T(8,128)(2,1)S(1)} %bitcast.9), channel_id=1, replica_groups={{11,1,15,12,6,13,10,14,4,3,8,0,5,2,7,9},{27,17,31,28,22,29,26,30,20,19,..., dimensions={0} | all-to-all | bytes 262144 | tf_op jit(solution)/shard_map/all_to_all | solution.py:254
  12.1 0.0 copy-done
  12.1 1.8 %shard_map.66 = bf16[1024,128]{1,0:T(8,128)(2,1)} custom-call(bf16[256,256]{1,0:T(8,128)(2,1)S(1)} %bitcast.8, bf16[3,256,256]{2,1,0:T(8,128)(2,1)S(1)} %get-tuple-element.12.hot_ref, bf16[6912,128]{1,0:T(8,128)(2,1)S(1)} %bitcast.7, f32[1,128]{1,0:T(1,128)S(1)} %get-tuple-element.13.bias_ref, f32[2,8,128]{2,1,0:T(8,128)S(1)} %get-tuple-element.14.mix_ref), custom_call_target="tpu_custom_call" | custom-call | tf_op jit(solution)/shard_map/pallas_call | solution.py:255
Async XLA Ops:
  1.0 11.2 %copy-start = (bf16[3,3,3,256,128]{4,3,2,1,0:T(8,128)(2,1)S(1)}, bf16[3,3,3,256,128]{4,3,2,1,0:T(8,128)(2,1)}, u32[]{:S(2)}) copy-start(bf16[3,3,3,256,128]{4,3,2,1,0:T(8,128)(2,1)} %param.8) | copy-start | bytes 5308420

commit v8 on v7

--- a/solution.py
+++ b/solution.py
@@ -95,7 +95,7 @@
     x_ref, take_ref, hot_ref, mix_ref, bias_ref, order_ref, ids_ref, table_ref, sems,
 ):
     moves = [
-        (order_hbm, order_ref), (x_hbm, x_ref), (ids_hbm, ids_ref), (table_hbm, table_ref), (bias_hbm, bias_ref),
+        (ids_hbm, ids_ref), (table_hbm, table_ref), (order_hbm, order_ref), (x_hbm, x_ref), (bias_hbm, bias_ref),
     ]
     copies = [pltpu.make_async_copy(a, b, sems.at[n]) for n, (a, b) in enumerate(moves)]
     for copy in copies:
@@ -103,14 +103,15 @@
     take_ref[...] = windows_hot(tiles, *take_ref.shape[::-1])
     rows, cols = hot_ref.shape[1:]
     wants = wanted_keys(rows, order_ref.shape[1])
-    copies[0].wait()
+    for copy in copies[:2]:
+        copy.wait()
+    mix_ref[0], mix_ref[1] = blend_mix(tiles, at_ref[0], ids_ref, table_ref, mix_ref.shape[1:])
+    copies[2].wait()
     key = jnp.broadcast_to(line_key(tiles, order_ref[...], cols), (rows, cols))
     for kw in range(3):
         hot_ref[kw] = (key == wants[kw]).astype(jnp.bfloat16)
-    for copy in copies[2:]:
-        copy.wait()
-    mix_ref[0], mix_ref[1] = blend_mix(tiles, at_ref[0], ids_ref, table_ref, mix_ref.shape[1:])
-    copies[1].wait()
+    copies[4].wait()
+    copies[3].wait()
 
 
 def windows_kernel(x_ref, take_ref, send_ref):
@@ -123,7 +124,8 @@
 
 
 def silu(value):
-    return 0.5 * value * (1.0 + jnp.tanh(0.5 * value))
+    half = 0.5 * value
+    return half + half * jnp.tanh(half)
 
 
 def decode_kernel(rows_ref, hot_ref, w_ref, bias_ref, mix_ref, out_hbm, part_ref, out_ref, sems):

time: 14.1 us -> 14.2 us (level)
  no operation moved by 1% of the time
where the time goes in v8:
time: 14.2 us; the launch traced here: 14 us
  blocking collectives  11 us (77%)
  Pallas kernels  2.97 us (21%)
    all_to_all x1, blocking collectives, per_device(): lax.all_to_all(send, 'tile', 0, 0, axis_index_groups=[list(order_of(tiles...  11 us
    pallas_call x1, Pallas kernels, per_device(): pl.pallas_call(decode_kernel, out_shape=jax.ShapeDtypeStruct((4 * LT * fr...  1.83 us
    pallas_call x1, Pallas kernels, per_device(): pl.pallas_call(functools.partial(prepare_kernel, tiles), out_shape=(pltpu...  0.98 us

profile of v8, /device:TPU:0, one launch (start us, length us, event | category | flops | bytes accessed | tf_op | source)
XLA Modules:
  0.0 14.0 jit_solution(4242544304392679658)
XLA Ops:
  0.0 1.0 %shard_map.64 = (bf16[128,256]{1,0:T(8,128)(2,1)S(1)}, bf16[256,128]{1,0:T(8,128)(2,1)S(1)}, bf16[3,256,256]{2,1,0:T(8,128)(2,1)S(1)}, f32[2,8,128]{2,1,0:T(8,128)S(1)}, f32[1,128]{1,0:T(1,128)S(1)}) custom-call(bf16[128,256]{1,0:T(8,128)(2,1)} %x_hbm.1, s32[1,64]{1,0:T(1,128)} %bitcast.10, s32[16]{0:T(128)} %ids_hbm.1, f32[4,8]{1,0:T(4,128)} %table_hbm.1, ...), custom_call_target="tpu_custom_call" | custom-call | tf_op jit(solution)/shard_map/pallas_call | solution.py:228
  1.0 0.0 copy-start
  1.0 0.2 %shard_map.65 = bf16[256,256]{1,0:T(8,128)(2,1)S(1)} custom-call(bf16[128,256]{1,0:T(8,128)(2,1)S(1)} %get-tuple-element.10.x_ref, bf16[256,128]{1,0:T(8,128)(2,1)S(1)} %get-tuple-element.11.take_ref), custom_call_target="tpu_custom_call" | custom-call | flops 10000000000 | bytes 10000000 | tf_op jit(solution)/shard_map/pallas_call | solution.py:249
  1.2 11.0 %all_to_all.11 = bf16[16,16,256]{2,1,0:T(8,128)(2,1)S(1)} all-to-all(bf16[16,16,256]{2,1,0:T(8,128)(2,1)S(1)} %bitcast.9), channel_id=1, replica_groups={{11,1,15,12,6,13,10,14,4,3,8,0,5,2,7,9},{27,17,31,28,22,29,26,30,20,19,..., dimensions={0} | all-to-all | bytes 262144 | tf_op jit(solution)/shard_map/all_to_all | solution.py:256
  12.2 0.0 copy-done
  12.2 1.8 %shard_map.66 = bf16[1024,128]{1,0:T(8,128)(2,1)} custom-call(bf16[256,256]{1,0:T(8,128)(2,1)S(1)} %bitcast.8, bf16[3,256,256]{2,1,0:T(8,128)(2,1)S(1)} %get-tuple-element.12.hot_ref, bf16[6912,128]{1,0:T(8,128)(2,1)S(1)} %bitcast.7, f32[1,128]{1,0:T(1,128)S(1)} %get-tuple-element.13.bias_ref, f32[2,8,128]{2,1,0:T(8,128)S(1)} %get-tuple-element.14.mix_ref), custom_call_target="tpu_custom_call" | custom-call | tf_op jit(solution)/shard_map/pallas_call | solution.py:257
Async XLA Ops:
  1.0 11.2 %copy-start = (bf16[3,3,3,256,128]{4,3,2,1,0:T(8,128)(2,1)S(1)}, bf16[3,3,3,256,128]{4,3,2,1,0:T(8,128)(2,1)}, u32[]{:S(2)}) copy-start(bf16[3,3,3,256,128]{4,3,2,1,0:T(8,128)(2,1)} %param.8) | copy-start | bytes 5308420

commit v9 on v8

--- a/solution.py
+++ b/solution.py
@@ -91,11 +91,11 @@
 
 
 def prepare_kernel(
-    tiles, x_hbm, order_hbm, ids_hbm, table_hbm, bias_hbm, at_ref,
-    x_ref, take_ref, hot_ref, mix_ref, bias_ref, order_ref, ids_ref, table_ref, sems,
+    tiles, x_hbm, order_hbm, ids_hbm, table_hbm, at_ref,
+    x_ref, take_ref, hot_ref, mix_ref, order_ref, ids_ref, table_ref, sems,
 ):
     moves = [
-        (ids_hbm, ids_ref), (table_hbm, table_ref), (order_hbm, order_ref), (x_hbm, x_ref), (bias_hbm, bias_ref),
+        (ids_hbm, ids_ref), (table_hbm, table_ref), (order_hbm, order_ref), (x_hbm, x_ref),
     ]
     copies = [pltpu.make_async_copy(a, b, sems.at[n]) for n, (a, b) in enumerate(moves)]
     for copy in copies:
@@ -110,7 +110,6 @@
     key = jnp.broadcast_to(line_key(tiles, order_ref[...], cols), (rows, cols))
     for kw in range(3):
         hot_ref[kw] = (key == wants[kw]).astype(jnp.bfloat16)
-    copies[4].wait()
     copies[3].wait()
 
 
@@ -225,25 +224,24 @@
     frame = lines // LT * 4
     count = LT * frame
     position = lax.axis_index("tile").astype(jnp.int32).reshape(1)
-    x, take, hot, mix, bias = pl.pallas_call(
+    x, take, hot, mix = pl.pallas_call(
         functools.partial(prepare_kernel, tiles),
         out_shape=(
             pltpu.VMEM((rows, depth), jnp.bfloat16),
             pltpu.VMEM((lines * span, rows), jnp.bfloat16),
             pltpu.VMEM((3, count, lines * span), jnp.bfloat16),
             pltpu.VMEM((2, 8, co), jnp.float32),
-            pltpu.VMEM((1, co), jnp.float32),
         ),
-        in_specs=[hbm()] * 5 + [smem()],
-        out_specs=(vmem(),) * 5,
+        in_specs=[hbm()] * 4 + [smem()],
+        out_specs=(vmem(),) * 4,
         scratch_shapes=[
             pltpu.VMEM((1, lines), jnp.int32),
             pltpu.SMEM(blend_ids.shape, jnp.int32),
             pltpu.SMEM(blend_table.shape, jnp.float32),
-            pltpu.SemaphoreType.DMA((5,)),
+            pltpu.SemaphoreType.DMA((4,)),
         ],
     )(
-        *map(outside, (latent_rows, line_order.reshape(1, -1), blend_ids, blend_table, conv_bias.reshape(1, co))),
+        *map(outside, (latent_rows, line_order.reshape(1, -1), blend_ids, blend_table)),
         position,
     )
     send = pl.pallas_call(
@@ -265,7 +263,7 @@
             pltpu.SemaphoreType.DMA((LT,)),
         ],
         compiler_params=pltpu.CompilerParams(vmem_limit_bytes=48 * 1024 * 1024),
-    )(held(received), held(hot), weights, held(bias), held(mix))
+    )(held(received), held(hot), weights, conv_bias.reshape(1, co), held(mix))
     return out.reshape(2 * LT, lines // LT * 2, 2 * WD, co)
 
 

time: 14.2 us -> 14.2 us (level)
  no operation moved by 1% of the time
where the time goes in v9:
time: 14.2 us; the launch traced here: 14 us
  blocking collectives  11 us (77%)
  Pallas kernels  2.97 us (21%)
    all_to_all x1, blocking collectives, per_device(): lax.all_to_all(send, 'tile', 0, 0, axis_index_groups=[list(order_of(tiles...  11 us
    pallas_call x1, Pallas kernels, per_device(): pl.pallas_call(decode_kernel, out_shape=jax.ShapeDtypeStruct((4 * LT * fr...  1.83 us
    pallas_call x1, Pallas kernels, per_device(): pl.pallas_call(functools.partial(prepare_kernel, tiles), out_shape=(pltpu...  0.97 us

profile of v9, /device:TPU:0, one launch (start us, length us, event | category | flops | bytes accessed | tf_op | source)
XLA Modules:
  0.0 14.0 jit_solution(7619426365005179303)
XLA Ops:
  0.0 1.0 %shard_map.64 = (bf16[128,256]{1,0:T(8,128)(2,1)S(1)}, bf16[256,128]{1,0:T(8,128)(2,1)S(1)}, bf16[3,256,256]{2,1,0:T(8,128)(2,1)S(1)}, f32[2,8,128]{2,1,0:T(8,128)S(1)}) custom-call(bf16[128,256]{1,0:T(8,128)(2,1)} %x_hbm.1, s32[1,64]{1,0:T(1,128)} %bitcast.11, s32[16]{0:T(128)} %ids_hbm.1, f32[4,8]{1,0:T(4,128)} %table_hbm.1, s32[1]{0:T(128)} %bitcast.1.at_ref), custom_call_target="tpu_custom_call" | custom-call | tf_op jit(solution)/shard_map/pallas_call | solution.py:227
  1.0 0.0 copy-start
  1.0 0.0 copy-start.1
  1.0 0.2 %shard_map.65 = bf16[256,256]{1,0:T(8,128)(2,1)S(1)} custom-call(bf16[128,256]{1,0:T(8,128)(2,1)S(1)} %get-tuple-element.9.x_ref, bf16[256,128]{1,0:T(8,128)(2,1)S(1)} %get-tuple-element.10.take_ref), custom_call_target="tpu_custom_call" | custom-call | flops 10000000000 | bytes 10000000 | tf_op jit(solution)/shard_map/pallas_call | solution.py:247
  1.2 11.0 %all_to_all.11 = bf16[16,16,256]{2,1,0:T(8,128)(2,1)S(1)} all-to-all(bf16[16,16,256]{2,1,0:T(8,128)(2,1)S(1)} %bitcast.9), channel_id=1, replica_groups={{11,1,15,12,6,13,10,14,4,3,8,0,5,2,7,9},{27,17,31,28,22,29,26,30,20,19,..., dimensions={0} | all-to-all | bytes 262144 | tf_op jit(solution)/shard_map/all_to_all | solution.py:254
  12.2 0.0 copy-done
  12.2 0.0 copy-done.1
  12.2 1.8 %shard_map.66 = bf16[1024,128]{1,0:T(8,128)(2,1)} custom-call(bf16[256,256]{1,0:T(8,128)(2,1)S(1)} %bitcast.8, bf16[3,256,256]{2,1,0:T(8,128)(2,1)S(1)} %get-tuple-element.11.hot_ref, bf16[6912,128]{1,0:T(8,128)(2,1)S(1)} %bitcast.7, f32[1,128]{1,0:T(1,128)S(1)} %bitcast.10, f32[2,8,128]{2,1,0:T(8,128)S(1)} %get-tuple-element.12.mix_ref), custom_call_target="tpu_custom_call" | custom-call | tf_op jit(solution)/shard_map/pallas_call | solution.py:255
Async XLA Ops:
  1.0 11.2 %copy-start = (bf16[3,3,3,256,128]{4,3,2,1,0:T(8,128)(2,1)S(1)}, bf16[3,3,3,256,128]{4,3,2,1,0:T(8,128)(2,1)}, u32[]{:S(2)}) copy-start(bf16[3,3,3,256,128]{4,3,2,1,0:T(8,128)(2,1)} %param.8) | copy-start | bytes 5308420
  1.0 11.2 %copy-start.1 = (f32[128]{0:T(128)S(1)}, f32[128]{0:T(128)}, u32[]{:S(2)}) copy-start(f32[128]{0:T(128)} %param.9) | copy-start | bytes 1540

commit v10 on v9

--- a/solution.py
+++ b/solution.py
@@ -10,7 +10,7 @@
 LT = 4
 WD = 2
 TAKES = ((0, 1, 1, 2), (1, 1, 2, 2), (1, 2, 2, 3))
-MEASURED = (11, 1, 15, 12, 6, 13, 10, 14, 4, 3, 8, 0, 5, 2, 7, 9)
+MEASURED = (11, 1, 15, 12, 2, 13, 4, 14, 10, 3, 8, 0, 5, 6, 7, 9)
 PACKED = ((1, 0, 2), (0, 0, 1), (0, 0, 2), (1, 1, 1), (1, 1, 2), (0, 1, 1), (0, 1, 2), (1, 0, 1))
 
 

time: 14.2 us -> 14.2 us (level)
  no operation moved by 1% of the time
where the time goes in v10:
time: 14.2 us; the launch traced here: 14 us
  blocking collectives  11 us (77%)
  Pallas kernels  2.97 us (21%)
    all_to_all x1, blocking collectives, per_device(): lax.all_to_all(send, 'tile', 0, 0, axis_index_groups=[list(order_of(tiles...  11 us
    pallas_call x1, Pallas kernels, per_device(): pl.pallas_call(decode_kernel, out_shape=jax.ShapeDtypeStruct((4 * LT * fr...  1.83 us
    pallas_call x1, Pallas kernels, per_device(): pl.pallas_call(functools.partial(prepare_kernel, tiles), out_shape=(pltpu...  0.97 us

profile of v10, /device:TPU:0, one launch (start us, length us, event | category | flops | bytes accessed | tf_op | source)
XLA Modules:
  0.0 14.0 jit_solution(16556803734267314543)
XLA Ops:
  0.0 1.0 %shard_map.64 = (bf16[128,256]{1,0:T(8,128)(2,1)S(1)}, bf16[256,128]{1,0:T(8,128)(2,1)S(1)}, bf16[3,256,256]{2,1,0:T(8,128)(2,1)S(1)}, f32[2,8,128]{2,1,0:T(8,128)S(1)}) custom-call(bf16[128,256]{1,0:T(8,128)(2,1)} %x_hbm.1, s32[1,64]{1,0:T(1,128)} %bitcast.11, s32[16]{0:T(128)} %ids_hbm.1, f32[4,8]{1,0:T(4,128)} %table_hbm.1, s32[1]{0:T(128)} %bitcast.1.at_ref), custom_call_target="tpu_custom_call" | custom-call | tf_op jit(solution)/shard_map/pallas_call | solution.py:227
  1.0 0.0 copy-start
  1.0 0.0 copy-start.1
  1.0 0.2 %shard_map.65 = bf16[256,256]{1,0:T(8,128)(2,1)S(1)} custom-call(bf16[128,256]{1,0:T(8,128)(2,1)S(1)} %get-tuple-element.9.x_ref, bf16[256,128]{1,0:T(8,128)(2,1)S(1)} %get-tuple-element.10.take_ref), custom_call_target="tpu_custom_call" | custom-call | flops 10000000000 | bytes 10000000 | tf_op jit(solution)/shard_map/pallas_call | solution.py:247
  1.2 11.0 %all_to_all.11 = bf16[16,16,256]{2,1,0:T(8,128)(2,1)S(1)} all-to-all(bf16[16,16,256]{2,1,0:T(8,128)(2,1)S(1)} %bitcast.9), channel_id=1, replica_groups={{11,1,15,12,2,13,4,14,10,3,8,0,5,6,7,9},{27,17,31,28,18,29,20,30,26,19,..., dimensions={0} | all-to-all | bytes 262144 | tf_op jit(solution)/shard_map/all_to_all | solution.py:254
  12.2 0.0 copy-done
  12.2 0.0 copy-done.1
  12.2 1.8 %shard_map.66 = bf16[1024,128]{1,0:T(8,128)(2,1)} custom-call(bf16[256,256]{1,0:T(8,128)(2,1)S(1)} %bitcast.8, bf16[3,256,256]{2,1,0:T(8,128)(2,1)S(1)} %get-tuple-element.11.hot_ref, bf16[6912,128]{1,0:T(8,128)(2,1)S(1)} %bitcast.7, f32[1,128]{1,0:T(1,128)S(1)} %bitcast.10, f32[2,8,128]{2,1,0:T(8,128)S(1)} %get-tuple-element.12.mix_ref), custom_call_target="tpu_custom_call" | custom-call | tf_op jit(solution)/shard_map/pallas_call | solution.py:255
Async XLA Ops:
  1.0 11.2 %copy-start = (bf16[3,3,3,256,128]{4,3,2,1,0:T(8,128)(2,1)S(1)}, bf16[3,3,3,256,128]{4,3,2,1,0:T(8,128)(2,1)}, u32[]{:S(2)}) copy-start(bf16[3,3,3,256,128]{4,3,2,1,0:T(8,128)(2,1)} %param.8) | copy-start | bytes 5308420
  1.0 11.2 %copy-start.1 = (f32[128]{0:T(128)S(1)}, f32[128]{0:T(128)}, u32[]{:S(2)}) copy-start(f32[128]{0:T(128)} %param.9) | copy-start | bytes 1540
